TPU v7x, 32 devices: a whole 2x2x4 slice. The times are simulated.
32 devices in a mesh: ctx: 8 (over z, y), tp: 4 (over x, core).
Axes of the slice: x: 2, y: 2, z: 4, core: 2. Of those that a mesh axis runs over, the one named last changes fastest.
Arguments:
- queries: bfloat16 [32, 128, 128], P('ctx', 'tp'), may hold values from -60 to 60
- cached_keys: bfloat16 [16384, 8, 128], P('ctx', 'tp'), may hold values from -6 to 6
- cached_values: bfloat16 [16384, 8, 128], P('ctx', 'tp'), may hold values from -6 to 6
- cached_pos: int32 [16384], P('ctx'), may hold values from -1 to 16383, as said below
- new_keys: bfloat16 [32, 8, 128], P('ctx', 'tp'), may hold values from -9 to 9
- new_values: bfloat16 [32, 8, 128], P('ctx', 'tp'), may hold values from -6 to 6
- new_pos: int32 [32], replicated, may hold values from 16384 to 16415, as said below
- out_weight: bfloat16 [16384, 16384], P('tp', 'ctx'), may hold values from -0.046875 to 0.046875
Outputs:
- context: bfloat16 [32, 16384], P('ctx', 'tp')
- projected: bfloat16 [32, 16384], P('tp', 'ctx')
Inputs may be any that keep to these rules, and one draw needn't show every extreme that they name: `cached_pos`: each index of ctx holds 2048 slots; the filled ones come first in its block, at least a quarter of them; some block is full; filled slots carry distinct positions below 16384. `new_pos`: distinct positions following the cache.
All inputs are finite; a program needn't handle non-finite values.
Results may differ from a plain program's by a relative error of at most 0.015.
Values may be sent and summed in bfloat16 or wider, within the bound.
A program may use at most 128 MiB of HBM per device.

v0:
```python
import math

import jax
import jax.numpy as jnp
from jax import lax
from jax.sharding import PartitionSpec as P

masked_score = -1e30


def tile(q4, keys, values, qpos, kpos, scale):
    s = jnp.einsum("rhgd,khd->rhgk", q4, keys, preferred_element_type=jnp.float32) * scale
    allow = ((kpos[None, :] >= 0) & (kpos[None, :] <= qpos[:, None]))[:, None, None, :]
    s = jnp.where(allow, s, masked_score)
    top = jnp.max(s, axis=-1)
    weights = jnp.where(allow, jnp.exp(s - top[..., None]), 0.0)
    total = jnp.sum(weights, axis=-1)
    numer = jnp.einsum(
        "rhgk,khd->rhgd", weights.astype(jnp.bfloat16), values, preferred_element_type=jnp.float32
    )
    return (numer, top, total)


def combine_parts(first, second):
    top = jnp.maximum(first[1], second[1])
    factor_a = jnp.exp(first[1] - top)
    factor_b = jnp.exp(second[1] - top)
    numer = first[0] * factor_a[..., None] + second[0] * factor_b[..., None]
    return (numer, top, first[2] * factor_a + second[2] * factor_b)


def per_device(
    queries, cached_keys, cached_values, cached_pos, new_keys, new_values, new_pos, out_weight
):
    local_new, heads, head_size = queries.shape
    slots, kv_heads = (cached_keys.shape[0], cached_keys.shape[1])
    group = heads // kv_heads
    scale = 1.0 / math.sqrt(head_size)
    block = math.gcd(slots, 512)
    nblk = slots // block
    key_blocks = cached_keys.reshape(nblk, block, kv_heads, head_size)
    value_blocks = cached_values.reshape(nblk, block, kv_heads, head_size)
    pos_blocks = cached_pos.reshape(nblk, block)
    own_pos = lax.dynamic_slice_in_dim(new_pos, lax.axis_index("ctx") * local_new, local_new)
    piece = lax.all_gather(queries, "ctx", axis=0, tiled=True)
    rows = piece.shape[0]
    q4 = piece.reshape(rows, kv_heads, group, head_size)
    init = (
        jnp.zeros((rows, kv_heads, group, head_size), jnp.float32),
        jnp.full((rows, kv_heads, group), masked_score, jnp.float32),
        jnp.zeros((rows, kv_heads, group), jnp.float32),
    )

    def step(carry, blk):
        return (combine_parts(carry, tile(q4, blk[0], blk[1], new_pos, blk[2], scale)), None)

    carry, _ = lax.scan(step, init, (key_blocks, value_blocks, pos_blocks))
    carry = combine_parts(carry, tile(q4, new_keys, new_values, new_pos, own_pos, scale))
    numer = carry[0].reshape(rows, heads, head_size)
    top = carry[1].reshape(rows, heads)
    total = carry[2].reshape(rows, heads)
    peak = lax.pmax(top.astype(jnp.bfloat16), "ctx").astype(top.dtype)
    factor = jnp.exp(top - peak)
    summed, weight_sum = (
        lax.psum_scatter(numer * factor[..., None], "ctx", scatter_dimension=0, tiled=True),
        lax.psum_scatter(total * factor, "ctx", scatter_dimension=0, tiled=True),
    )
    context = (
        (summed / weight_sum[..., None]).astype(jnp.bfloat16).reshape(local_new, heads * head_size)
    )
    terms = jnp.dot(
        lax.all_gather(context, "ctx", axis=0, tiled=True),
        out_weight,
        preferred_element_type=jnp.float32,
    )
    projected = lax.psum_scatter(terms.astype(jnp.bfloat16), "tp", scatter_dimension=0, tiled=True)
    return (context, projected)


def solution(mesh):
    in_specs = (
        P("ctx", "tp", None),
        P("ctx", "tp", None),
        P("ctx", "tp", None),
        P("ctx"),
        P("ctx", "tp", None),
        P("ctx", "tp", None),
        P(),
        P("tp", "ctx"),
    )
    out_specs = (P("ctx", "tp"), P("tp", "ctx"))
    return jax.shard_map(
        per_device, mesh=mesh, in_specs=in_specs, out_specs=out_specs, check_vma=False
    )
```

profile of v0, /device:TPU:0, one launch (start us, length us, event | category | flops | bytes accessed | tf_op | source)
XLA Modules:
  0.0 210.7 jit_solution(11053456104589304472)
XLA Ops:
  7.3 32.7 %all_gather.6 = bf16[32,32,128]{2,1,0:T(8,128)(2,1)S(1)} all-gather(bf16[4,32,128]{2,1,0:T(8,128)(2,1)} %param.10), channel_id=1, replica_groups=mesh['ctx'=8,'tp'=4] {'ctx'}, dimensions={0}, use_global_device_ids=true | all-gather | bytes 294912 | tf_op jit(solution)/shard_map/all_gather | solution.py:45
  40.8 0.7 broadcast_compare_fusion
  41.5 17.3 %while.15 = (s32[]{:T(128)}, f32[32,2,16,128]{3,0,2,1:T(8,128)S(1)}, f32[32,2,16]{0,2,1:T(8,128)S(1)}, f32[32,2,16]{0,2,1:T(8,128)S(1)}, s32[4,512]{1,0:T(4,128)...) while((s32[]{:T(128)}, ...), condition=%wide.region_3.4_spmd.clone, body=%wide.region_0.3_spmd.clone.sunk | while | flops 275814912 | bytes 9305344 | solution.py:57
  41.6 0.7 compare_and_fusion.3
  42.3 1.4 constant_dynamic-slice_fusion.6
  44.9 0.9 fusion.43
  45.9 0.7 compare_and_fusion.3
  46.7 1.4 constant_dynamic-slice_fusion.6
  49.3 0.9 fusion.43
  50.3 0.7 compare_and_fusion.3
  51.0 1.4 constant_dynamic-slice_fusion.6
  53.6 0.9 fusion.43
  54.6 0.7 compare_and_fusion.3
  55.3 1.4 constant_dynamic-slice_fusion.6
  57.9 0.9 fusion.43
  58.9 0.7 compare_and_fusion.1
  60.2 21.7 %pmax.7 = bf16[32,32]{0,1:T(8,128)(2,1)S(1)} all-reduce(bf16[32,32]{0,1:T(8,128)(2,1)S(1)} %bitcast_convert_fusion), channel_id=1, replica_groups=mesh['ctx'=8,'tp'=4] {'ctx'}, use_global_device_ids=true, to_apply=%region_5.6 | all-reduce | flops 1024 | bytes 4096 | tf_op jit(solution)/shard_map/pmax | solution.py:62
  82.9 1.0 bitcast_multiply_fusion
  85.3 33.0 %all-reduce = f32[32,32]{1,0:T(8,128)S(1)} all-reduce(f32[32,32]{1,0:T(8,128)S(1)} %copy.61), channel_id=3, replica_groups=mesh['ctx'=8,'tp'=4] {'ctx'}, use_global_device_ids=true, to_apply=%region_8.9.clone | all-reduce | flops 1024 | bytes 8192
  118.3 25.3 %reduce-scatter.3.cloned.1.call-done = f32[4,32,128]{2,1,0:T(8,128)} async-done(((f32[32,32,128]{2,1,0:T(8,128)}), f32[4,32,128]{2,1,0:T(8,128)}) %reduce-scatter.3.cloned.1.call-update) | async-done | bytes 65552 | tf_op jit(solution)/shard_map/reduce_scatter | solution.py:65
  143.7 0.9 divide_convert_fusion
  144.6 30.9 %all-gather = bf16[8,4,4096]{2,1,0:T(4,128)(2,1)S(1)} all-gather(bf16[1,4,4096]{2,1,0:T(4,128)(2,1)S(1)} %reshape.117), channel_id=1, replica_groups=mesh['ctx'=8,'tp'=4] {'ctx'}, dimensions={0}, use_global_device_ids=true | all-gather | bytes 294912 | tf_op jit(solution)/shard_map/all_gather | solution.py:72
  175.6 9.4 %convolution_convert_fusion = bf16[32,2048]{1,0:T(8,128)(2,1)} fusion(bf16[32,4096]{1,0:T(8,128)(2,1)S(1)} %reshape.118, bf16[4096,2048]{1,0:T(8,128)(2,1)} %param.17), kind=kOutput, calls=%fused_computation.29 | convolution fusion | flops 536936448 | bytes 17170432 | tf_op jit(solution)/shard_map/dot_general | solution.py:71
  185.8 18.1 %reduce-scatter.5.cloned.1.call-done = bf16[8,2048]{1,0:T(8,128)(2,1)} async-done(((bf16[32,2048]{1,0:T(8,128)(2,1)}), bf16[8,2048]{1,0:T(8,128)(2,1)}) %reduce-scatter.5.cloned.1.call-update) | async-done | bytes 32784 | tf_op jit(solution)/shard_map/reduce_scatter | solution.py:76
  (51 shorter events, 8.8 us)
Async XLA Ops:
  7.2 75.1 %copy-start = (bf16[4,2,128]{2,1,0:T(2,128)(2,1)S(1)}, bf16[4,2,128]{2,1,0:T(2,128)(2,1)}, u32[]{:S(2)}) copy-start(bf16[4,2,128]{2,1,0:T(2,128)(2,1)} %param.15) | copy-start | bytes 6148
  7.2 136.5 %reduce-scatter.3.cloned.1.call-start = ((), (), s32[]{:S(2)}) async-start(), calls=%async_computation.2 | async-start | bytes 589824 | tf_op jit(solution)/shard_map/reduce_scatter | solution.py:65
  41.5 18.1 %copy-start.2 = (bf16[4,2,128]{2,1,0:T(2,128)(2,1)S(1)}, bf16[4,2,128]{2,1,0:T(2,128)(2,1)}, u32[]{:S(2)}) copy-start(bf16[4,2,128]{2,1,0:T(2,128)(2,1)} %param.14) | copy-start | bytes 6148
  81.9 2.2 %copy-start.3 = (u32[32]{0:T(128)S(1)}, u32[32]{0:T(128)}, u32[]{:S(2)}) copy-start(u32[32]{0:T(128)} %constant.50) | copy-start | bytes 388
  83.9 120.0 %reduce-scatter.5.cloned.1.call-start = ((), (), s32[]{:S(2)}) async-start(), calls=%async_computation.3 | async-start | bytes 163840 | tf_op jit(solution)/shard_map/reduce_scatter | solution.py:76
  175.6 9.5 %copy-start.1 = (f32[4,32,128]{2,1,0:T(8,128)S(1)}, f32[4,32,128]{2,1,0:T(8,128)}, u32[]{:S(2)}) copy-start(f32[4,32,128]{2,1,0:T(8,128)} %reduce-scatter.3.cloned.1.call-done) | copy-start | bytes 196612
Sparse Core Ops, SparseCore 0:
  84.1 59.5 reduce-scatter.2
  185.2 18.6 reduce-scatter.4
where the time goes:
time: 211 us
  blocking collectives  118 us (56%)
  waiting for transfers between devices  43.4 us (21%)
  matrix products  16.2 us (8%)
  between operations  14.9 us (7%)
  other arithmetic  9.36 us (4%)
  local copies, waits for them, and re-layouts  8.21 us (4%)
    unnamed x1, blocking collectives  33 us
    all_gather x1, blocking collectives, per_device(): piece = lax.all_gather(queries, 'ctx', axis=0, tiled=True)  32.7 us
    all_gather x1, blocking collectives, per_device(): lax.all_gather(context, 'ctx', axis=0, tiled=True)  30.9 us
    reduce_scatter x1, waiting for transfers between devices, per_device(): lax.psum_scatter(numer * factor[..., None], 'ctx', scatter_dimension=0, t...  25.3 us
    pmax x1, blocking collectives, per_device(): peak = lax.pmax(top.astype(jnp.bfloat16), 'ctx').astype(top.dtype)  21.7 us
    reduce_scatter x1, waiting for transfers between devices, per_device(): lax.psum_scatter(terms.astype(jnp.bfloat16), 'tp', scatter_dimension=0, t...  18.1 us
    dot_general x1, matrix products, per_device(): jnp.dot(lax.all_gather(context, 'ctx', axis=0, tiled=True), out_weight, p...  9.44 us
    dynamic_slice x4, local copies, waits for them, and re-layouts, per_device(): carry, _ = lax.scan(step, init, (key_blocks, value_blocks, pos_blocks))  5.6 us
  transfers between devices with their start and end apart: 2, of which 2 were waited for; matrix products, arithmetic and copies ran while one was open for 1% of the time, Pallas kernels for 0%

commit v1 on v0

v1 whole, which is shorter than its diff:
```python
import functools
import math

import jax
import jax.numpy as jnp
from jax import lax
from jax.experimental import pallas as pl
from jax.experimental.pallas import tpu as pltpu
from jax.sharding import PartitionSpec as P

masked_score = -1e30
MESH = pl.DeviceIdType.MESH
lanes = 128
new_pad = 128
col_tiles = 4
bf16 = jnp.bfloat16
f32 = jnp.float32


def kernel(
    n, ntp, local_new, kv_heads, group, slots,
    q_ref, k_hbm, v_hbm, pos_ref, nk_ref, nv_ref, newpos_ref, w_hbm,
    ctx_out, proj_out,
    kraw, vraw, kh, vh, wide, small, bias_c, bias_n, qall, wbuf,
    onum, rnum, sstat, rstat, wts, cown, call, cf, lhs, acc, dsend, drecv,
    k_sem, v_sem, w_sem, q_send, q_recv, n_send, n_recv, s_send, s_recv,
    c_send, c_recv, d_send, d_recv,
):
    me = lax.axis_index("ctx")
    tp = lax.axis_index("tp")
    rows = local_new * group
    per_chunk = lanes // rows
    chunks = n // per_chunk
    mine = me // per_chunk
    tokens = n * local_new
    depth = group * lanes
    coef = math.log2(math.e) / math.sqrt(lanes)

    k_copy = pltpu.make_async_copy(k_hbm, kraw, k_sem)
    v_copy = pltpu.make_async_copy(v_hbm, vraw, v_sem)
    k_copy.start()
    v_copy.start()
    w_parts = 4 * kv_heads
    w_rows = kv_heads * depth // w_parts
    w_copies = [
        pltpu.make_async_copy(
            w_hbm.at[pl.ds(i * w_rows, w_rows)], wbuf.at[pl.ds(i * w_rows, w_rows)], w_sem.at[i]
        )
        for i in range(w_parts)
    ]
    for copy in w_copies:
        copy.start()

    barrier = pltpu.get_barrier_semaphore()

    def greet(i, _):
        pl.semaphore_signal(
            barrier, inc=1, device_id={"ctx": lax.rem(me + i, n)}, device_id_type=MESH
        )
        return 0

    lax.fori_loop(1, n, greet, 0)
    for i in range(1, ntp):
        pl.semaphore_signal(
            barrier, inc=1, device_id={"tp": lax.rem(tp + i, ntp)}, device_id_type=MESH
        )
    pl.semaphore_wait(barrier, n - 1 + ntp - 1)

    def q_copy(slot, peer):
        return pltpu.make_async_remote_copy(
            src_ref=q_ref,
            dst_ref=qall.at[pl.ds(slot * local_new, local_new)],
            send_sem=q_send.at[peer],
            recv_sem=q_recv.at[slot],
            device_id={"ctx": peer},
            device_id_type=MESH,
        )

    def num_copy(h, peer, slot):
        return pltpu.make_async_remote_copy(
            src_ref=onum.at[h, peer],
            dst_ref=rnum.at[h, slot],
            send_sem=n_send.at[h, peer],
            recv_sem=n_recv.at[h, slot],
            device_id={"ctx": peer},
            device_id_type=MESH,
        )

    def stat_copy(h, peer, slot):
        return pltpu.make_async_remote_copy(
            src_ref=sstat.at[h, peer // per_chunk],
            dst_ref=rstat.at[pl.ds((h * n + slot) * 8, 8)],
            send_sem=s_send.at[h, peer],
            recv_sem=s_recv.at[h, slot],
            device_id={"ctx": peer},
            device_id_type=MESH,
        )

    def ctx_copy(h, peer, slot):
        return pltpu.make_async_remote_copy(
            src_ref=call.at[h, slot],
            dst_ref=call.at[h, slot],
            send_sem=c_send.at[h, peer],
            recv_sem=c_recv.at[h, slot],
            device_id={"ctx": peer},
            device_id_type=MESH,
        )

    def part_copy(j, peer, slot):
        return pltpu.make_async_remote_copy(
            src_ref=dsend.at[j, peer],
            dst_ref=drecv.at[j, slot],
            send_sem=d_send.at[j, peer],
            recv_sem=d_recv.at[j, slot],
            device_id={"tp": peer},
            device_id_type=MESH,
        )

    def others(body):
        def step(i, _):
            body(lax.rem(me + i, n))
            return 0

        lax.fori_loop(1, n, step, 0)

    def send_queries(i, _):
        c = lax.rem(mine + chunks - i, chunks)
        for j in range(per_chunk):
            peer = c * per_chunk + j

            @pl.when(peer != me)
            def _():
                q_copy(me, peer).start()

        return 0

    lax.fori_loop(0, chunks, send_queries, 0)
    qall[pl.ds(me * local_new, local_new)] = q_ref[...]

    bias_c[...] = jnp.where(pos_ref[...] >= 0, 0.0, masked_score)
    lane = lax.broadcasted_iota(jnp.int32, (group, lanes), 1)
    key_pos = jnp.full((group, lanes), 2**30, jnp.int32)
    for j in range(local_new):
        key_pos = jnp.where(lane == j, newpos_ref[me * local_new + j], key_pos)

    def mask_new(t, _):
        bias_n[pl.ds(t * group, group), :] = jnp.where(
            key_pos <= newpos_ref[t], 0.0, masked_score
        )
        return 0

    lax.fori_loop(0, tokens, mask_new, 0)

    part = math.gcd(slots, 256)

    def split_heads(raw, new_ref, out):
        def step(i, _):
            wide[...] = raw[pl.ds(i * part * kv_heads, part * kv_heads), :].astype(f32)
            for h in range(kv_heads):
                out[h, pl.ds(i * part, part), :] = wide[
                    pl.ds(h, part, stride=kv_heads), :
                ].astype(bf16)
            return 0

        lax.fori_loop(0, slots // part, step, 0)
        wide[pl.ds(0, local_new * kv_heads), :] = new_ref[...].astype(f32)
        for h in range(kv_heads):
            small[...] = jnp.zeros_like(small)
            small[pl.ds(0, local_new), :] = wide[pl.ds(h, local_new, stride=kv_heads), :]
            out[h, pl.ds(slots, new_pad), :] = small[...].astype(bf16)

    k_copy.wait()
    split_heads(kraw, nk_ref, kh)
    v_copy.wait()
    split_heads(vraw, nv_ref, vh)

    diag = lax.broadcasted_iota(jnp.int32, (lanes, lanes), 0) == lax.broadcasted_iota(
        jnp.int32, (lanes, lanes), 1
    )

    def attend(h):
        def step(i, _):
            c = lax.rem(mine + i, chunks)
            if h == 0:
                for j in range(per_chunk):
                    peer = c * per_chunk + j

                    @pl.when(peer != me)
                    def _():
                        q_copy(peer, peer).wait_recv()

            tok = c * per_chunk * local_new
            q = qall[pl.ds(tok, per_chunk * local_new), pl.ds(h * group, group), :]
            q = q.reshape(lanes, lanes)
            s = lax.dot_general(
                q, kh[h], (((1,), (1,)), ((), ())), preferred_element_type=f32
            )
            old = s[:, :slots] + bias_c[...]
            new = s[:, slots:] + bias_n[pl.ds(tok * group, lanes), :]
            top = jnp.maximum(
                jnp.max(old, axis=1, keepdims=True), jnp.max(new, axis=1, keepdims=True)
            )
            old = jnp.exp2((old - top) * coef)
            new = jnp.exp2((new - top) * coef)
            total = jnp.sum(old, axis=1, keepdims=True) + jnp.sum(new, axis=1, keepdims=True)
            out = jnp.dot(old.astype(bf16), vh[h, :slots], preferred_element_type=f32)
            out += jnp.dot(new.astype(bf16), vh[h, slots:], preferred_element_type=f32)
            out = (out / total).astype(bf16)
            level = top * coef + jnp.log2(total)
            stat = jnp.sum(jnp.where(diag, level, 0.0), axis=0, keepdims=True)
            stat = jnp.broadcast_to(stat, (8, lanes))
            sstat[h, c] = stat
            for j in range(per_chunk):
                peer = c * per_chunk + j
                onum[h, peer] = out[j * rows : (j + 1) * rows]

                @pl.when(peer != me)
                def _():
                    stat_copy(h, peer, me).start()
                    num_copy(h, peer, me).start()

                @pl.when(peer == me)
                def _():
                    rnum[h, me] = out[j * rows : (j + 1) * rows]
                    rstat[pl.ds((h * n + me) * 8, 8), :] = stat

            return 0

        lax.fori_loop(0, chunks, step, 0)

    def combine(h):
        def arrived(peer):
            stat_copy(h, peer, peer).wait_recv()
            num_copy(h, peer, peer).wait_recv()

        others(arrived)
        level = rstat[pl.ds(h * n * 8, n, stride=8), :]
        factor = jnp.exp2(level - jnp.max(level, axis=0, keepdims=True))
        factor = factor / jnp.sum(factor, axis=0, keepdims=True)
        wts[...] = factor.T
        first = pl.multiple_of(lax.rem(me, per_chunk) * rows, rows)
        weight = wts[pl.ds(first, rows), :]
        context = jnp.zeros((rows, lanes), f32)
        for s in range(n):
            context += rnum[h, s].astype(f32) * weight[:, s : s + 1]
        call[h, me] = context.astype(bf16)
        others(lambda peer: ctx_copy(h, peer, me).start())
        cown[...] = context
        for g in range(group):
            at = (h * group + g) * lanes
            ctx_out[:, at : at + lanes] = cown[pl.ds(g, local_new, stride=group), :].astype(bf16)

    tile = proj_out.shape[1] // col_tiles
    half = tile // 2
    block = tokens // ntp

    def project(h):
        others(lambda peer: ctx_copy(h, peer, peer).wait_recv())
        cf[...] = call[h].reshape(tokens * group, lanes).astype(f32)
        for g in range(group):
            lhs[:, g * lanes : (g + 1) * lanes] = cf[pl.ds(g, tokens, stride=group), :].astype(bf16)
        for copy in w_copies[h * 4 : (h + 1) * 4]:
            copy.wait()
        for j in range(col_tiles):
            cols = slice(j * tile, (j + 1) * tile)
            term = jnp.dot(
                lhs[...], wbuf[h * depth : (h + 1) * depth, cols], preferred_element_type=f32
            )
            if h > 0:
                term += acc[:, cols]
            if h < kv_heads - 1:
                acc[:, cols] = term
                continue
            for r in range(ntp):
                slab = term[r * block : (r + 1) * block]
                slab = jnp.concatenate([slab[:, :half], slab[:, half:]], axis=0).astype(bf16)
                dsend[j, r] = slab

                @pl.when(tp != r)
                def _():
                    part_copy(j, r, tp).start()

                @pl.when(tp == r)
                def _():
                    drecv[j, tp] = slab

    for h in range(kv_heads):
        attend(h)
    for h in range(kv_heads):
        combine(h)
    for h in range(kv_heads):
        project(h)

    for j in range(col_tiles):
        for i in range(1, ntp):
            peer = lax.rem(tp + i, ntp)
            part_copy(j, peer, peer).wait_recv()
        total = drecv[j, 0].astype(f32)
        for r in range(1, ntp):
            total += drecv[j, r].astype(f32)
        proj_out[:, j * tile : (j + 1) * tile] = jnp.concatenate(
            [total[:block], total[block:]], axis=1
        ).astype(bf16)

    def sent(peer):
        q_copy(me, peer).wait_send()
        for h in range(kv_heads):
            num_copy(h, peer, me).wait_send()
            stat_copy(h, peer, me).wait_send()
            ctx_copy(h, peer, me).wait_send()

    others(sent)
    for j in range(col_tiles):
        for i in range(1, ntp):
            part_copy(j, lax.rem(tp + i, ntp), tp).wait_send()


def per_device(
    n, ntp, queries, cached_keys, cached_values, cached_pos, new_keys, new_values, new_pos,
    out_weight,
):
    local_new, heads, head_size = queries.shape
    slots, kv_heads = cached_keys.shape[:2]
    group = heads // kv_heads
    rows = local_new * group
    tokens = n * local_new
    depth, cols = out_weight.shape
    chunks = n // (lanes // rows)
    all_keys = slots + new_pad
    block = tokens // ntp
    half = cols // col_tiles // 2
    vmem = pl.BlockSpec(memory_space=pltpu.VMEM)
    hbm = pl.BlockSpec(memory_space=pl.ANY)
    dma = pltpu.SemaphoreType.DMA
    flops = 4 * tokens * heads * slots * head_size + 2 * tokens * depth * cols
    return pl.pallas_call(
        functools.partial(kernel, n, ntp, local_new, kv_heads, group, slots),
        out_shape=(
            jax.ShapeDtypeStruct((local_new, depth), bf16),
            jax.ShapeDtypeStruct((block, cols), bf16),
        ),
        in_specs=[vmem, hbm, hbm, vmem, vmem, vmem, pl.BlockSpec(memory_space=pltpu.SMEM), hbm],
        out_specs=(vmem, vmem),
        scratch_shapes=[
            pltpu.VMEM((slots * kv_heads, lanes), bf16),
            pltpu.VMEM((slots * kv_heads, lanes), bf16),
            pltpu.VMEM((kv_heads, all_keys, lanes), bf16),
            pltpu.VMEM((kv_heads, all_keys, lanes), bf16),
            pltpu.VMEM((math.gcd(slots, 256) * kv_heads, lanes), f32),
            pltpu.VMEM((new_pad, lanes), f32),
            pltpu.VMEM((1, slots), f32),
            pltpu.VMEM((tokens * group, lanes), f32),
            pltpu.VMEM((tokens, heads, lanes), bf16),
            pltpu.VMEM((depth, cols), bf16),
            pltpu.VMEM((kv_heads, n, rows, lanes), bf16),
            pltpu.VMEM((kv_heads, n, rows, lanes), bf16),
            pltpu.VMEM((kv_heads, chunks, 8, lanes), f32),
            pltpu.VMEM((kv_heads * n * 8, lanes), f32),
            pltpu.VMEM((lanes, n), f32),
            pltpu.VMEM((rows, lanes), f32),
            pltpu.VMEM((kv_heads, n, rows, lanes), bf16),
            pltpu.VMEM((tokens * group, lanes), f32),
            pltpu.VMEM((tokens, group * lanes), bf16),
            pltpu.VMEM((tokens, cols), f32),
            pltpu.VMEM((col_tiles, ntp, 2 * block, half), bf16),
            pltpu.VMEM((col_tiles, ntp, 2 * block, half), bf16),
            dma, dma, dma((4 * kv_heads,)),
            dma((n,)), dma((n,)),
            dma((kv_heads, n)), dma((kv_heads, n)),
            dma((kv_heads, n)), dma((kv_heads, n)),
            dma((kv_heads, n)), dma((kv_heads, n)),
            dma((col_tiles, ntp)), dma((col_tiles, ntp)),
        ],
        compiler_params=pltpu.CompilerParams(
            collective_id=0, has_side_effects=True, vmem_limit_bytes=56 * 2**20
        ),
        cost_estimate=pl.CostEstimate(
            flops=flops,
            bytes_accessed=2 * depth * cols + 4 * slots * kv_heads * head_size,
            transcendentals=tokens * heads * slots,
        ),
    )(
        queries,
        cached_keys.reshape(slots * kv_heads, head_size),
        cached_values.reshape(slots * kv_heads, head_size),
        cached_pos.reshape(1, slots),
        new_keys.reshape(local_new * kv_heads, head_size),
        new_values.reshape(local_new * kv_heads, head_size),
        new_pos,
        out_weight,
    )


def solution(mesh):
    in_specs = (
        P("ctx", "tp", None),
        P("ctx", "tp", None),
        P("ctx", "tp", None),
        P("ctx"),
        P("ctx", "tp", None),
        P("ctx", "tp", None),
        P(),
        P("tp", "ctx"),
    )
    out_specs = (P("ctx", "tp"), P("tp", "ctx"))
    return jax.shard_map(
        functools.partial(per_device, mesh.shape["ctx"], mesh.shape["tp"]),
        mesh=mesh, in_specs=in_specs, out_specs=out_specs, check_vma=False,
    )
```

time: 211 us -> 41.1 us (0.19)
  blocking collectives: 118 us -> 0 us
  waiting for transfers between devices: 43.4 us -> 0 us
  Pallas kernels: 0 us -> 37.4 us
  matrix products: 16.2 us -> 0 us
  between operations: 14.9 us -> 0.64 us
  other arithmetic: 9.36 us -> 0 us
  local copies, waits for them, and re-layouts: 8.21 us -> 2.76 us
    all_gather x2 -> x0, blocking collectives: 63.7 us -> none  [the longest x1 32.7 us: per_device(): piece = lax.all_gather(queries, 'ctx', axis=0, tiled=True)]
    reduce_scatter x2 -> x0, waiting for transfers between devices: 43.4 us -> none  [the longest x1 25.3 us: per_device(): lax.psum_scatter(numer * factor[..., None], 'ctx', scatter_dimension=0, t...]
    pallas_call x0 -> x1, Pallas kernels: none -> 37.4 us  [per_device(): pl.pallas_call(functools.partial(kernel, n, ntp, local_new, kv_heads, gro...]
    unnamed x1 -> x0, blocking collectives: 33 us -> none
    pmax x1 -> x0, blocking collectives: 21.7 us -> none  [per_device(): peak = lax.pmax(top.astype(jnp.bfloat16), 'ctx').astype(top.dtype)]
    dot_general x11 -> x0, matrix products: 16.2 us -> none  [the longest x1 9.44 us: per_device(): jnp.dot(lax.all_gather(context, 'ctx', axis=0, tiled=True), out_weight, p...]
    dynamic_slice x4 -> x0, local copies, waits for them, and re-layouts: 5.6 us -> none  [per_device(): carry, _ = lax.scan(step, init, (key_blocks, value_blocks, pos_blocks))]
    and x5 -> x0, other arithmetic: 3.69 us -> none  [tile(): (kpos[None, :] >= 0) & (kpos[None, :] <= qpos[:, None])]
  transfers between devices with their start and end apart: 2 -> 0, of which waited for: 2 -> 0; matrix products, arithmetic and copies ran while one was open for 1% -> 0% of each run, Pallas kernels for 0% -> 0%
where the time goes in v1:
time: 41.1 us; the launch traced here: 40.8 us
  Pallas kernels  37.4 us (91%)
  local copies, waits for them, and re-layouts  2.76 us (7%)
  between operations  0.64 us (2%)
    pallas_call x1, Pallas kernels, per_device(): pl.pallas_call(functools.partial(kernel, n, ntp, local_new, kv_heads, gro...  37.4 us
    unnamed x2, local copies, waits for them, and re-layouts  2.76 us

profile of v1, /device:TPU:0, one launch (start us, length us, event | category | flops | bytes accessed | tf_op | source)
XLA Modules:
  0.0 40.8 jit_solution(8409372663164208521)
XLA Ops:
  0.6 37.4 %shard_map.95 = (bf16[4,4096]{1,0:T(4,128)(2,1)}, bf16[8,2048]{1,0:T(8,128)(2,1)}) custom-call(bf16[4,32,128]{2,1,0:T(8,128)(2,1)} %q_ref.1, bf16[4096,128]{1,0:T(8,128)(2,1)} %bitcast.5, bf16[4096,128]{1,0:T(8,128)(2,1)} %bitcast.6, s32[1,2048]{1,0:T(1,128)} %bitcast.7, bf16[8,128]{1,0:T(8,128)(2,1)} %bitcast.8, bf16[8,128]{1,0:T(8,128)(2,1)} %bitcast.9, ...), custom_call_target="tpu_custom_call" | custom-call | flops 1610612736 | bytes 18874368 | tf_op jit(solution)/shard_map/pallas_call | solution.py:336
  38.0 1.4 %copy.12 = bf16[4,4096]{1,0:T(4,128)(2,1)} copy(bf16[4,4096]{1,0:T(4,128)(2,1)} %get-tuple-element.4) | data formatting | bytes 65536
  39.4 1.4 %copy.13 = bf16[8,2048]{1,0:T(8,128)(2,1)} copy(bf16[8,2048]{1,0:T(8,128)(2,1)} %get-tuple-element.5) | data formatting | bytes 65536

commit v2 on v1

--- a/solution.py
+++ b/solution.py
@@ -19,11 +19,11 @@
 
 def kernel(
     n, ntp, local_new, kv_heads, group, slots,
-    q_ref, k_hbm, v_hbm, pos_ref, nk_ref, nv_ref, newpos_ref, w_hbm,
-    ctx_out, proj_out,
+    q_hbm, k_hbm, v_hbm, pos_hbm, nk_hbm, nv_hbm, newpos_hbm, w_hbm,
+    ctx_out, proj_out, pos_ref, nk_ref, nv_ref, newpos_ref,
     kraw, vraw, kh, vh, wide, small, bias_c, bias_n, qall, wbuf,
     onum, rnum, sstat, rstat, wts, cown, call, cf, lhs, acc, dsend, drecv,
-    k_sem, v_sem, w_sem, q_send, q_recv, n_send, n_recv, s_send, s_recv,
+    k_sem, v_sem, i_sem, w_sem, q_send, q_recv, n_send, n_recv, s_send, s_recv,
     c_send, c_recv, d_send, d_recv,
 ):
     me = lax.axis_index("ctx")
@@ -38,6 +38,18 @@
 
     k_copy = pltpu.make_async_copy(k_hbm, kraw, k_sem)
     v_copy = pltpu.make_async_copy(v_hbm, vraw, v_sem)
+    small_copies = [
+        pltpu.make_async_copy(src, dst, i_sem.at[i])
+        for i, (src, dst) in enumerate(
+            [(newpos_hbm, newpos_ref), (pos_hbm, pos_ref), (nk_hbm, nk_ref), (nv_hbm, nv_ref)]
+        )
+    ]
+    own_q = pltpu.make_async_copy(
+        q_hbm, qall.at[pl.ds(me * local_new, local_new)], i_sem.at[4]
+    )
+    for copy in small_copies:
+        copy.start()
+    own_q.start()
     k_copy.start()
     v_copy.start()
     w_parts = 4 * kv_heads
@@ -48,8 +60,6 @@
         )
         for i in range(w_parts)
     ]
-    for copy in w_copies:
-        copy.start()
 
     barrier = pltpu.get_barrier_semaphore()
 
@@ -64,11 +74,27 @@
         pl.semaphore_signal(
             barrier, inc=1, device_id={"tp": lax.rem(tp + i, ntp)}, device_id_type=MESH
         )
+    for copy in small_copies:
+        copy.wait()
+    bias_c[...] = jnp.where(pos_ref[...] >= 0, 0.0, masked_score)
+    lane = lax.broadcasted_iota(jnp.int32, (group, lanes), 1)
+    key_pos = jnp.full((group, lanes), 2**30, jnp.int32)
+    for j in range(local_new):
+        key_pos = jnp.where(lane == j, newpos_ref[me * local_new + j], key_pos)
+
+    def mask_new(t, _):
+        bias_n[pl.ds(t * group, group), :] = jnp.where(
+            key_pos <= newpos_ref[t], 0.0, masked_score
+        )
+        return 0
+
+    lax.fori_loop(0, tokens, mask_new, 0)
+
     pl.semaphore_wait(barrier, n - 1 + ntp - 1)
 
     def q_copy(slot, peer):
         return pltpu.make_async_remote_copy(
-            src_ref=q_ref,
+            src_ref=q_hbm,
             dst_ref=qall.at[pl.ds(slot * local_new, local_new)],
             send_sem=q_send.at[peer],
             recv_sem=q_recv.at[slot],
@@ -135,23 +161,8 @@
         return 0
 
     lax.fori_loop(0, chunks, send_queries, 0)
-    qall[pl.ds(me * local_new, local_new)] = q_ref[...]
-
-    bias_c[...] = jnp.where(pos_ref[...] >= 0, 0.0, masked_score)
-    lane = lax.broadcasted_iota(jnp.int32, (group, lanes), 1)
-    key_pos = jnp.full((group, lanes), 2**30, jnp.int32)
-    for j in range(local_new):
-        key_pos = jnp.where(lane == j, newpos_ref[me * local_new + j], key_pos)
-
-    def mask_new(t, _):
-        bias_n[pl.ds(t * group, group), :] = jnp.where(
-            key_pos <= newpos_ref[t], 0.0, masked_score
-        )
-        return 0
-
-    lax.fori_loop(0, tokens, mask_new, 0)
-
-    part = math.gcd(slots, 256)
+
+    part = math.gcd(slots, 512)
 
     def split_heads(raw, new_ref, out):
         def step(i, _):
@@ -170,31 +181,32 @@
             out[h, pl.ds(slots, new_pad), :] = small[...].astype(bf16)
 
     k_copy.wait()
+    v_copy.wait()
+    for copy in w_copies:
+        copy.start()
     split_heads(kraw, nk_ref, kh)
-    v_copy.wait()
     split_heads(vraw, nv_ref, vh)
+    own_q.wait()
 
     diag = lax.broadcasted_iota(jnp.int32, (lanes, lanes), 0) == lax.broadcasted_iota(
         jnp.int32, (lanes, lanes), 1
     )
 
-    def attend(h):
-        def step(i, _):
-            c = lax.rem(mine + i, chunks)
-            if h == 0:
-                for j in range(per_chunk):
-                    peer = c * per_chunk + j
-
-                    @pl.when(peer != me)
-                    def _():
-                        q_copy(peer, peer).wait_recv()
-
-            tok = c * per_chunk * local_new
+    def attend(c, others_of_chunk):
+        tok = c * per_chunk * local_new
+        for peer in others_of_chunk:
+            q_copy(peer, peer).wait_recv()
+        scores = []
+        for h in range(kv_heads):
             q = qall[pl.ds(tok, per_chunk * local_new), pl.ds(h * group, group), :]
-            q = q.reshape(lanes, lanes)
-            s = lax.dot_general(
-                q, kh[h], (((1,), (1,)), ((), ())), preferred_element_type=f32
+            scores.append(
+                lax.dot_general(
+                    q.reshape(lanes, lanes), kh[h], (((1,), (1,)), ((), ())),
+                    preferred_element_type=f32,
+                )
             )
+        for h in range(kv_heads):
+            s = scores[h]
             old = s[:, :slots] + bias_c[...]
             new = s[:, slots:] + bias_n[pl.ds(tok * group, lanes), :]
             top = jnp.maximum(
@@ -208,25 +220,31 @@
             out = (out / total).astype(bf16)
             level = top * coef + jnp.log2(total)
             stat = jnp.sum(jnp.where(diag, level, 0.0), axis=0, keepdims=True)
-            stat = jnp.broadcast_to(stat, (8, lanes))
-            sstat[h, c] = stat
+            sstat[h, c] = jnp.broadcast_to(stat, (8, lanes))
             for j in range(per_chunk):
-                peer = c * per_chunk + j
-                onum[h, peer] = out[j * rows : (j + 1) * rows]
-
-                @pl.when(peer != me)
-                def _():
-                    stat_copy(h, peer, me).start()
-                    num_copy(h, peer, me).start()
-
-                @pl.when(peer == me)
-                def _():
-                    rnum[h, me] = out[j * rows : (j + 1) * rows]
-                    rstat[pl.ds((h * n + me) * 8, 8), :] = stat
-
+                onum[h, c * per_chunk + j] = out[j * rows : (j + 1) * rows]
+        for h in range(kv_heads):
+            for peer in others_of_chunk:
+                stat_copy(h, peer, me).start()
+                num_copy(h, peer, me).start()
+
+    def attend_all():
+        attend(
+            mine,
+            [
+                mine * per_chunk + lax.rem(me + j, per_chunk) for j in range(1, per_chunk)
+            ],
+        )
+        for h in range(kv_heads):
+            rnum[h, me] = onum[h, me]
+            rstat[pl.ds((h * n + me) * 8, 8), :] = sstat[h, mine]
+
+        def step(i, _):
+            c = lax.rem(mine + i, chunks)
+            attend(c, [c * per_chunk + j for j in range(per_chunk)])
             return 0
 
-        lax.fori_loop(0, chunks, step, 0)
+        lax.fori_loop(1, chunks, step, 0)
 
     def combine(h):
         def arrived(peer):
@@ -284,8 +302,7 @@
                 def _():
                     drecv[j, tp] = slab
 
-    for h in range(kv_heads):
-        attend(h)
+    attend_all()
     for h in range(kv_heads):
         combine(h)
     for h in range(kv_heads):
@@ -313,6 +330,17 @@
     for j in range(col_tiles):
         for i in range(1, ntp):
             part_copy(j, lax.rem(tp + i, ntp), tp).wait_send()
+
+
+def deliver(ctx_in, proj_in, ctx_out, proj_out, sem):
+    copies = [
+        pltpu.make_async_copy(ctx_in, ctx_out, sem.at[0]),
+        pltpu.make_async_copy(proj_in, proj_out, sem.at[1]),
+    ]
+    for copy in copies:
+        copy.start()
+    for copy in copies:
+        copy.wait()
 
 
 def per_device(
@@ -333,20 +361,25 @@
     hbm = pl.BlockSpec(memory_space=pl.ANY)
     dma = pltpu.SemaphoreType.DMA
     flops = 4 * tokens * heads * slots * head_size + 2 * tokens * depth * cols
-    return pl.pallas_call(
-        functools.partial(kernel, n, ntp, local_new, kv_heads, group, slots),
-        out_shape=(
+    out_shape = (
             jax.ShapeDtypeStruct((local_new, depth), bf16),
             jax.ShapeDtypeStruct((block, cols), bf16),
-        ),
-        in_specs=[vmem, hbm, hbm, vmem, vmem, vmem, pl.BlockSpec(memory_space=pltpu.SMEM), hbm],
+        )
+    context, projected = pl.pallas_call(
+        functools.partial(kernel, n, ntp, local_new, kv_heads, group, slots),
+        out_shape=out_shape,
+        in_specs=[hbm] * 8,
         out_specs=(vmem, vmem),
         scratch_shapes=[
+            pltpu.VMEM((1, slots), jnp.int32),
+            pltpu.VMEM((local_new * kv_heads, lanes), bf16),
+            pltpu.VMEM((local_new * kv_heads, lanes), bf16),
+            pltpu.SMEM((tokens,), jnp.int32),
             pltpu.VMEM((slots * kv_heads, lanes), bf16),
             pltpu.VMEM((slots * kv_heads, lanes), bf16),
             pltpu.VMEM((kv_heads, all_keys, lanes), bf16),
             pltpu.VMEM((kv_heads, all_keys, lanes), bf16),
-            pltpu.VMEM((math.gcd(slots, 256) * kv_heads, lanes), f32),
+            pltpu.VMEM((math.gcd(slots, 512) * kv_heads, lanes), f32),
             pltpu.VMEM((new_pad, lanes), f32),
             pltpu.VMEM((1, slots), f32),
             pltpu.VMEM((tokens * group, lanes), f32),
@@ -364,7 +397,7 @@
             pltpu.VMEM((tokens, cols), f32),
             pltpu.VMEM((col_tiles, ntp, 2 * block, half), bf16),
             pltpu.VMEM((col_tiles, ntp, 2 * block, half), bf16),
-            dma, dma, dma((4 * kv_heads,)),
+            dma, dma, dma((5,)), dma((4 * kv_heads,)),
             dma((n,)), dma((n,)),
             dma((kv_heads, n)), dma((kv_heads, n)),
             dma((kv_heads, n)), dma((kv_heads, n)),
@@ -389,6 +422,14 @@
         new_pos,
         out_weight,
     )
+    return pl.pallas_call(
+        deliver,
+        out_shape=out_shape,
+        in_specs=[hbm, hbm],
+        out_specs=(hbm, hbm),
+        scratch_shapes=[dma((2,))],
+        compiler_params=pltpu.CompilerParams(vmem_limit_bytes=60 * 2**20),
+    )(context, projected)
 
 
 def solution(mesh):

time: 41.1 us -> 39.7 us (0.966)
  local copies, waits for them, and re-layouts: 2.76 us -> 0 us
  Pallas kernels: 37.4 us -> 38.9 us
    pallas_call x0 -> x1, Pallas kernels: none -> 3.11 us  [per_device(): pl.pallas_call(deliver, out_shape=out_shape, in_specs=[hbm, hbm], out_spe...]
    unnamed x2 -> x0, local copies, waits for them, and re-layouts: 2.76 us -> none
    pallas_call x1, Pallas kernels: 37.4 us -> 35.8 us  [per_device(): pl.pallas_call(functools.partial(kernel, n, ntp, local_new, kv_heads, gro...]
where the time goes in v2:
time: 39.7 us; the launch traced here: 39.5 us
  Pallas kernels  38.9 us (98%)
  between operations  0.64 us (2%)
    pallas_call x1, Pallas kernels, per_device(): pl.pallas_call(functools.partial(kernel, n, ntp, local_new, kv_heads, gro...  35.8 us
    pallas_call x1, Pallas kernels, per_device(): pl.pallas_call(deliver, out_shape=out_shape, in_specs=[hbm, hbm], out_spe...  3.11 us

profile of v2, /device:TPU:0, one launch (start us, length us, event | category | flops | bytes accessed | tf_op | source)
XLA Modules:
  0.0 39.5 jit_solution(16376077074229161194)
XLA Ops:
  0.6 35.8 %shard_map.95 = (bf16[4,4096]{1,0:T(4,128)(2,1)}, bf16[8,2048]{1,0:T(8,128)(2,1)}) custom-call(bf16[4,32,128]{2,1,0:T(8,128)(2,1)} %q_hbm.1, bf16[4096,128]{1,0:T(8,128)(2,1)} %bitcast.5, bf16[4096,128]{1,0:T(8,128)(2,1)} %bitcast.6, s32[1,2048]{1,0:T(1,128)} %bitcast.7, bf16[8,128]{1,0:T(8,128)(2,1)} %bitcast.8, bf16[8,128]{1,0:T(8,128)(2,1)} %bitcast.9, ...), custom_call_target="tpu_custom_call" | custom-call | flops 1610612736 | bytes 18874368 | tf_op jit(solution)/shard_map/pallas_call | solution.py:368
  36.4 3.1 %shard_map.96 = (bf16[4,4096]{1,0:T(4,128)(2,1)}, bf16[8,2048]{1,0:T(8,128)(2,1)}) custom-call(bf16[4,4096]{1,0:T(4,128)(2,1)} %get-tuple-element.4.ctx_in, bf16[8,2048]{1,0:T(8,128)(2,1)} %get-tuple-element.5.proj_in), custom_call_target="tpu_custom_call" | custom-call | tf_op jit(solution)/shard_map/pallas_call | solution.py:425

commit v3 on v2

--- a/solution.py
+++ b/solution.py
@@ -32,6 +32,10 @@
     per_chunk = lanes // rows
     chunks = n // per_chunk
     mine = me // per_chunk
+    outer = n // 2
+    hi = me // 2
+    lo = lax.rem(me, 2)
+    mate = hi * 2 + 1 - lo
     tokens = n * local_new
     depth = group * lanes
     coef = math.log2(math.e) / math.sqrt(lanes)
@@ -92,11 +96,12 @@
 
     pl.semaphore_wait(barrier, n - 1 + ntp - 1)
 
-    def q_copy(slot, peer):
+    def q_copy(slot, peer, sem):
+        part = qall.at[pl.ds(slot * local_new, local_new)]
         return pltpu.make_async_remote_copy(
-            src_ref=q_hbm,
-            dst_ref=qall.at[pl.ds(slot * local_new, local_new)],
-            send_sem=q_send.at[peer],
+            src_ref=part,
+            dst_ref=part,
+            send_sem=q_send.at[sem],
             recv_sem=q_recv.at[slot],
             device_id={"ctx": peer},
             device_id_type=MESH,
@@ -122,11 +127,11 @@
             device_id_type=MESH,
         )
 
-    def ctx_copy(h, peer, slot):
+    def ctx_copy(h, peer, slot, sem):
         return pltpu.make_async_remote_copy(
             src_ref=call.at[h, slot],
             dst_ref=call.at[h, slot],
-            send_sem=c_send.at[h, peer],
+            send_sem=c_send.at[h, sem],
             recv_sem=c_recv.at[h, slot],
             device_id={"ctx": peer},
             device_id_type=MESH,
@@ -149,18 +154,20 @@
 
         lax.fori_loop(1, n, step, 0)
 
-    def send_queries(i, _):
-        c = lax.rem(mine + chunks - i, chunks)
-        for j in range(per_chunk):
-            peer = c * per_chunk + j
-
-            @pl.when(peer != me)
-            def _():
-                q_copy(me, peer).start()
-
-        return 0
-
-    lax.fori_loop(0, chunks, send_queries, 0)
+    def peers(first, last, body):
+        def step(i, _):
+            body(lax.rem(hi + i, outer) * 2 + lo)
+            return 0
+
+        lax.fori_loop(first, last, step, 0)
+
+    own_q.wait()
+    q_copy(me, mate, mate).start()
+    peers(1, outer, lambda peer: q_copy(me, peer, peer).start())
+
+    def pass_queries(slot):
+        q_copy(slot, slot, slot).wait_recv()
+        q_copy(slot, mate, slot + 1 - 2 * lo).start()
 
     part = math.gcd(slots, 512)
 
@@ -185,8 +192,9 @@
     for copy in w_copies:
         copy.start()
     split_heads(kraw, nk_ref, kh)
+    peers(outer - 1, outer, pass_queries)
     split_heads(vraw, nv_ref, vh)
-    own_q.wait()
+    peers(1, outer - 1, pass_queries)
 
     diag = lax.broadcasted_iota(jnp.int32, (lanes, lanes), 0) == lax.broadcasted_iota(
         jnp.int32, (lanes, lanes), 1
@@ -194,8 +202,16 @@
 
     def attend(c, others_of_chunk):
         tok = c * per_chunk * local_new
-        for peer in others_of_chunk:
-            q_copy(peer, peer).wait_recv()
+        if per_chunk % 2 == 0:
+            for j in range(per_chunk // 2):
+                slot = c * per_chunk + 2 * j + 1 - lo
+                q_copy(slot, slot, slot).wait_recv()
+        else:
+
+            @pl.when(lax.rem(c, 2) != lo)
+            def _():
+                q_copy(c, c, c).wait_recv()
+
         scores = []
         for h in range(kv_heads):
             q = qall[pl.ds(tok, per_chunk * local_new), pl.ds(h * group, group), :]
@@ -240,7 +256,7 @@
             rstat[pl.ds((h * n + me) * 8, 8), :] = sstat[h, mine]
 
         def step(i, _):
-            c = lax.rem(mine + i, chunks)
+            c = lax.rem(mine + chunks - i, chunks)
             attend(c, [c * per_chunk + j for j in range(per_chunk)])
             return 0
 
@@ -262,18 +278,31 @@
         for s in range(n):
             context += rnum[h, s].astype(f32) * weight[:, s : s + 1]
         call[h, me] = context.astype(bf16)
-        others(lambda peer: ctx_copy(h, peer, me).start())
+        peers(1, outer, lambda peer: ctx_copy(h, peer, me, peer).start())
+        ctx_copy(h, mate, me, mate).start()
         cown[...] = context
         for g in range(group):
             at = (h * group + g) * lanes
             ctx_out[:, at : at + lanes] = cown[pl.ds(g, local_new, stride=group), :].astype(bf16)
 
+    def relay(h):
+        def body(slot):
+            ctx_copy(h, slot, slot, slot).wait_recv()
+            ctx_copy(h, mate, slot, slot + 1 - 2 * lo).start()
+
+        peers(1, outer, body)
+
     tile = proj_out.shape[1] // col_tiles
     half = tile // 2
     block = tokens // ntp
 
     def project(h):
-        others(lambda peer: ctx_copy(h, peer, peer).wait_recv())
+        def from_mate(i, _):
+            slot = i * 2 + 1 - lo
+            ctx_copy(h, slot, slot, slot).wait_recv()
+            return 0
+
+        lax.fori_loop(0, outer, from_mate, 0)
         cf[...] = call[h].reshape(tokens * group, lanes).astype(f32)
         for g in range(group):
             lhs[:, g * lanes : (g + 1) * lanes] = cf[pl.ds(g, tokens, stride=group), :].astype(bf16)
@@ -306,6 +335,8 @@
     for h in range(kv_heads):
         combine(h)
     for h in range(kv_heads):
+        relay(h)
+    for h in range(kv_heads):
         project(h)
 
     for j in range(col_tiles):
@@ -320,11 +351,11 @@
         ).astype(bf16)
 
     def sent(peer):
-        q_copy(me, peer).wait_send()
+        q_copy(me, peer, peer).wait_send()
         for h in range(kv_heads):
             num_copy(h, peer, me).wait_send()
             stat_copy(h, peer, me).wait_send()
-            ctx_copy(h, peer, me).wait_send()
+            ctx_copy(h, peer, me, peer).wait_send()
 
     others(sent)
     for j in range(col_tiles):
@@ -332,15 +363,9 @@
             part_copy(j, lax.rem(tp + i, ntp), tp).wait_send()
 
 
-def deliver(ctx_in, proj_in, ctx_out, proj_out, sem):
-    copies = [
-        pltpu.make_async_copy(ctx_in, ctx_out, sem.at[0]),
-        pltpu.make_async_copy(proj_in, proj_out, sem.at[1]),
-    ]
-    for copy in copies:
-        copy.start()
-    for copy in copies:
-        copy.wait()
+def deliver(ctx_in, proj_in, ctx_out, proj_out):
+    ctx_out[...] = ctx_in[...]
+    proj_out[...] = proj_in[...]
 
 
 def per_device(
@@ -425,10 +450,8 @@
     return pl.pallas_call(
         deliver,
         out_shape=out_shape,
-        in_specs=[hbm, hbm],
-        out_specs=(hbm, hbm),
-        scratch_shapes=[dma((2,))],
-        compiler_params=pltpu.CompilerParams(vmem_limit_bytes=60 * 2**20),
+        in_specs=[vmem, vmem],
+        out_specs=(vmem, vmem),
     )(context, projected)
 
 

time: 39.7 us -> 39 us (0.982)
  Pallas kernels: 38.9 us -> 38.1 us
    pallas_call x1, Pallas kernels: 3.11 us -> 1.4 us  [per_device(): pl.pallas_call(deliver, out_shape=out_shape, in_specs=[vmem, vmem], out_s...]
    pallas_call x1, Pallas kernels: 35.8 us -> 36.7 us  [per_device(): pl.pallas_call(functools.partial(kernel, n, ntp, local_new, kv_heads, gro...]
where the time goes in v3:
time: 39 us; the launch traced here: 38.8 us
  Pallas kernels  38.1 us (98%)
  between operations  0.64 us (2%)
    pallas_call x1, Pallas kernels, per_device(): pl.pallas_call(functools.partial(kernel, n, ntp, local_new, kv_heads, gro...  36.7 us
    pallas_call x1, Pallas kernels, per_device(): pl.pallas_call(deliver, out_shape=out_shape, in_specs=[vmem, vmem], out_s...  1.4 us

profile of v3, /device:TPU:0, one launch (start us, length us, event | category | flops | bytes accessed | tf_op | source)
XLA Modules:
  0.0 38.8 jit_solution(13533162063617361458)
XLA Ops:
  0.6 36.7 %shard_map.95 = (bf16[4,4096]{1,0:T(4,128)(2,1)}, bf16[8,2048]{1,0:T(8,128)(2,1)}) custom-call(bf16[4,32,128]{2,1,0:T(8,128)(2,1)} %q_hbm.1, bf16[4096,128]{1,0:T(8,128)(2,1)} %bitcast.5, bf16[4096,128]{1,0:T(8,128)(2,1)} %bitcast.6, s32[1,2048]{1,0:T(1,128)} %bitcast.7, bf16[8,128]{1,0:T(8,128)(2,1)} %bitcast.8, bf16[8,128]{1,0:T(8,128)(2,1)} %bitcast.9, ...), custom_call_target="tpu_custom_call" | custom-call | flops 1610612736 | bytes 18874368 | tf_op jit(solution)/shard_map/pallas_call | solution.py:393
  37.4 1.4 %shard_map.96 = (bf16[4,4096]{1,0:T(4,128)(2,1)}, bf16[8,2048]{1,0:T(8,128)(2,1)}) custom-call(bf16[4,4096]{1,0:T(4,128)(2,1)} %get-tuple-element.4.ctx_in, bf16[8,2048]{1,0:T(8,128)(2,1)} %get-tuple-element.5.proj_in), custom_call_target="tpu_custom_call" | custom-call | tf_op jit(solution)/shard_map/pallas_call | solution.py:450

commit v4 on v2

--- a/solution.py
+++ b/solution.py
@@ -12,7 +12,8 @@
 MESH = pl.DeviceIdType.MESH
 lanes = 128
 new_pad = 128
-col_tiles = 4
+col_tiles = 2
+stat_rows = 16
 bf16 = jnp.bfloat16
 f32 = jnp.float32
 
@@ -22,8 +23,8 @@
     q_hbm, k_hbm, v_hbm, pos_hbm, nk_hbm, nv_hbm, newpos_hbm, w_hbm,
     ctx_out, proj_out, pos_ref, nk_ref, nv_ref, newpos_ref,
     kraw, vraw, kh, vh, wide, small, bias_c, bias_n, qall, wbuf,
-    onum, rnum, sstat, rstat, wts, cown, call, cf, lhs, acc, dsend, drecv,
-    k_sem, v_sem, i_sem, w_sem, q_send, q_recv, n_send, n_recv, s_send, s_recv,
+    onum, rnum, stat, wts, cown, call, cf, lhs, acc, dsend, drecv,
+    k_sem, v_sem, i_sem, w_sem, q_send, q_recv, n_send, n_recv,
     c_send, c_recv, d_send, d_recv,
 ):
     me = lax.axis_index("ctx")
@@ -32,6 +33,7 @@
     per_chunk = lanes // rows
     chunks = n // per_chunk
     mine = me // per_chunk
+    num_rows = kv_heads * rows
     tokens = n * local_new
     depth = group * lanes
     coef = math.log2(math.e) / math.sqrt(lanes)
@@ -92,55 +94,48 @@
 
     pl.semaphore_wait(barrier, n - 1 + ntp - 1)
 
-    def q_copy(slot, peer):
+    def q_copy(peer):
         return pltpu.make_async_remote_copy(
             src_ref=q_hbm,
-            dst_ref=qall.at[pl.ds(slot * local_new, local_new)],
-            send_sem=q_send.at[peer],
-            recv_sem=q_recv.at[slot],
+            dst_ref=qall.at[pl.ds(me * local_new, local_new)],
+            send_sem=q_send,
+            recv_sem=q_recv.at[mine],
             device_id={"ctx": peer},
             device_id_type=MESH,
         )
 
-    def num_copy(h, peer, slot):
+    def num_copy(peer):
         return pltpu.make_async_remote_copy(
-            src_ref=onum.at[h, peer],
-            dst_ref=rnum.at[h, slot],
-            send_sem=n_send.at[h, peer],
-            recv_sem=n_recv.at[h, slot],
+            src_ref=onum.at[peer],
+            dst_ref=rnum.at[me],
+            send_sem=n_send,
+            recv_sem=n_recv,
             device_id={"ctx": peer},
             device_id_type=MESH,
         )
 
-    def stat_copy(h, peer, slot):
+    def ctx_copy(h, peer):
         return pltpu.make_async_remote_copy(
-            src_ref=sstat.at[h, peer // per_chunk],
-            dst_ref=rstat.at[pl.ds((h * n + slot) * 8, 8)],
-            send_sem=s_send.at[h, peer],
-            recv_sem=s_recv.at[h, slot],
+            src_ref=call.at[h, me],
+            dst_ref=call.at[h, me],
+            send_sem=c_send.at[h],
+            recv_sem=c_recv.at[h],
             device_id={"ctx": peer},
             device_id_type=MESH,
         )
 
-    def ctx_copy(h, peer, slot):
-        return pltpu.make_async_remote_copy(
-            src_ref=call.at[h, slot],
-            dst_ref=call.at[h, slot],
-            send_sem=c_send.at[h, peer],
-            recv_sem=c_recv.at[h, slot],
-            device_id={"ctx": peer},
-            device_id_type=MESH,
-        )
-
-    def part_copy(j, peer, slot):
+    def part_copy(j, peer):
         return pltpu.make_async_remote_copy(
             src_ref=dsend.at[j, peer],
-            dst_ref=drecv.at[j, slot],
-            send_sem=d_send.at[j, peer],
-            recv_sem=d_recv.at[j, slot],
+            dst_ref=drecv.at[j, tp],
+            send_sem=d_send.at[j],
+            recv_sem=d_recv.at[j],
             device_id={"tp": peer},
             device_id_type=MESH,
         )
+
+    def await_bytes(ref, sem):
+        pltpu.make_async_copy(ref, ref, sem).wait()
 
     def others(body):
         def step(i, _):
@@ -149,18 +144,20 @@
 
         lax.fori_loop(1, n, step, 0)
 
+    def chunk_at(i, sign):
+        shift = lax.rem(i + chunks // 2 - 2, chunks - 1) + 1
+        return lax.rem(mine + chunks + sign * shift, chunks)
+
+    for j in range(1, per_chunk):
+        q_copy(mine * per_chunk + lax.rem(me + j, per_chunk)).start()
+
     def send_queries(i, _):
-        c = lax.rem(mine + chunks - i, chunks)
+        c = chunk_at(i, 1)
         for j in range(per_chunk):
-            peer = c * per_chunk + j
-
-            @pl.when(peer != me)
-            def _():
-                q_copy(me, peer).start()
-
+            q_copy(c * per_chunk + j).start()
         return 0
 
-    lax.fori_loop(0, chunks, send_queries, 0)
+    lax.fori_loop(1, chunks, send_queries, 0)
 
     part = math.gcd(slots, 512)
 
@@ -188,14 +185,16 @@
     split_heads(vraw, nv_ref, vh)
     own_q.wait()
 
+    stat_row = lax.broadcasted_iota(jnp.int32, (stat_rows, lanes), 0)
     diag = lax.broadcasted_iota(jnp.int32, (lanes, lanes), 0) == lax.broadcasted_iota(
         jnp.int32, (lanes, lanes), 1
     )
 
     def attend(c, others_of_chunk):
         tok = c * per_chunk * local_new
-        for peer in others_of_chunk:
-            q_copy(peer, peer).wait_recv()
+        arrivals = len(others_of_chunk) * local_new
+        if arrivals > 0:
+            await_bytes(qall.at[pl.ds(0, arrivals)], q_recv.at[c])
         scores = []
         for h in range(kv_heads):
             q = qall[pl.ds(tok, per_chunk * local_new), pl.ds(h * group, group), :]
@@ -205,6 +204,7 @@
                     preferred_element_type=f32,
                 )
             )
+        levels = jnp.zeros((stat_rows, lanes), f32)
         for h in range(kv_heads):
             s = scores[h]
             old = s[:, :slots] + bias_c[...]
@@ -219,14 +219,19 @@
             out += jnp.dot(new.astype(bf16), vh[h, slots:], preferred_element_type=f32)
             out = (out / total).astype(bf16)
             level = top * coef + jnp.log2(total)
-            stat = jnp.sum(jnp.where(diag, level, 0.0), axis=0, keepdims=True)
-            sstat[h, c] = jnp.broadcast_to(stat, (8, lanes))
+            level = jnp.sum(jnp.where(diag, level, 0.0), axis=0, keepdims=True)
+            for k in range(3):
+                piece = level.astype(bf16).astype(f32)
+                level = level - piece
+                levels = jnp.where(stat_row == 3 * h + k, piece, levels)
             for j in range(per_chunk):
-                onum[h, c * per_chunk + j] = out[j * rows : (j + 1) * rows]
-        for h in range(kv_heads):
-            for peer in others_of_chunk:
-                stat_copy(h, peer, me).start()
-                num_copy(h, peer, me).start()
+                onum[c * per_chunk + j, h * rows : (h + 1) * rows] = out[
+                    j * rows : (j + 1) * rows
+                ]
+        for j in range(per_chunk):
+            onum[c * per_chunk + j, num_rows:] = levels.astype(bf16)
+        for peer in others_of_chunk:
+            num_copy(peer).start()
 
     def attend_all():
         attend(
@@ -235,24 +240,19 @@
                 mine * per_chunk + lax.rem(me + j, per_chunk) for j in range(1, per_chunk)
             ],
         )
-        for h in range(kv_heads):
-            rnum[h, me] = onum[h, me]
-            rstat[pl.ds((h * n + me) * 8, 8), :] = sstat[h, mine]
+        rnum[me] = onum[me]
 
         def step(i, _):
-            c = lax.rem(mine + i, chunks)
+            c = chunk_at(i, -1)
             attend(c, [c * per_chunk + j for j in range(per_chunk)])
             return 0
 
         lax.fori_loop(1, chunks, step, 0)
 
     def combine(h):
-        def arrived(peer):
-            stat_copy(h, peer, peer).wait_recv()
-            num_copy(h, peer, peer).wait_recv()
-
-        others(arrived)
-        level = rstat[pl.ds(h * n * 8, n, stride=8), :]
+        level = stat[pl.ds(3 * h, n, stride=stat_rows), :]
+        for k in range(1, 3):
+            level += stat[pl.ds(3 * h + k, n, stride=stat_rows), :]
         factor = jnp.exp2(level - jnp.max(level, axis=0, keepdims=True))
         factor = factor / jnp.sum(factor, axis=0, keepdims=True)
         wts[...] = factor.T
@@ -260,9 +260,9 @@
         weight = wts[pl.ds(first, rows), :]
         context = jnp.zeros((rows, lanes), f32)
         for s in range(n):
-            context += rnum[h, s].astype(f32) * weight[:, s : s + 1]
+            context += rnum[s, h * rows : (h + 1) * rows].astype(f32) * weight[:, s : s + 1]
         call[h, me] = context.astype(bf16)
-        others(lambda peer: ctx_copy(h, peer, me).start())
+        others(lambda peer: ctx_copy(h, peer).start())
         cown[...] = context
         for g in range(group):
             at = (h * group + g) * lanes
@@ -273,7 +273,7 @@
     block = tokens // ntp
 
     def project(h):
-        others(lambda peer: ctx_copy(h, peer, peer).wait_recv())
+        await_bytes(call.at[h, pl.ds(0, n - 1)], c_recv.at[h])
         cf[...] = call[h].reshape(tokens * group, lanes).astype(f32)
         for g in range(group):
             lhs[:, g * lanes : (g + 1) * lanes] = cf[pl.ds(g, tokens, stride=group), :].astype(bf16)
@@ -296,22 +296,22 @@
 
                 @pl.when(tp != r)
                 def _():
-                    part_copy(j, r, tp).start()
+                    part_copy(j, r).start()
 
                 @pl.when(tp == r)
                 def _():
                     drecv[j, tp] = slab
 
     attend_all()
+    await_bytes(rnum.at[pl.ds(0, n - 1)], n_recv)
+    stat[...] = rnum[:, num_rows:, :].reshape(n * stat_rows, lanes).astype(f32)
     for h in range(kv_heads):
         combine(h)
     for h in range(kv_heads):
         project(h)
 
     for j in range(col_tiles):
-        for i in range(1, ntp):
-            peer = lax.rem(tp + i, ntp)
-            part_copy(j, peer, peer).wait_recv()
+        await_bytes(drecv.at[j, pl.ds(0, ntp - 1)], d_recv.at[j])
         total = drecv[j, 0].astype(f32)
         for r in range(1, ntp):
             total += drecv[j, r].astype(f32)
@@ -319,28 +319,17 @@
             [total[:block], total[block:]], axis=1
         ).astype(bf16)
 
-    def sent(peer):
-        q_copy(me, peer).wait_send()
-        for h in range(kv_heads):
-            num_copy(h, peer, me).wait_send()
-            stat_copy(h, peer, me).wait_send()
-            ctx_copy(h, peer, me).wait_send()
-
-    others(sent)
+    await_bytes(qall.at[pl.ds(0, (n - 1) * local_new)], q_send)
+    await_bytes(onum.at[pl.ds(0, n - 1)], n_send)
+    for h in range(kv_heads):
+        await_bytes(call.at[h, pl.ds(0, n - 1)], c_send.at[h])
     for j in range(col_tiles):
-        for i in range(1, ntp):
-            part_copy(j, lax.rem(tp + i, ntp), tp).wait_send()
-
-
-def deliver(ctx_in, proj_in, ctx_out, proj_out, sem):
-    copies = [
-        pltpu.make_async_copy(ctx_in, ctx_out, sem.at[0]),
-        pltpu.make_async_copy(proj_in, proj_out, sem.at[1]),
-    ]
-    for copy in copies:
-        copy.start()
-    for copy in copies:
-        copy.wait()
+        await_bytes(dsend.at[j, pl.ds(0, ntp - 1)], d_send.at[j])
+
+
+def deliver(ctx_in, proj_in, ctx_out, proj_out):
+    ctx_out[...] = ctx_in[...]
+    proj_out[...] = proj_in[...]
 
 
 def per_device(
@@ -385,10 +374,9 @@
             pltpu.VMEM((tokens * group, lanes), f32),
             pltpu.VMEM((tokens, heads, lanes), bf16),
             pltpu.VMEM((depth, cols), bf16),
-            pltpu.VMEM((kv_heads, n, rows, lanes), bf16),
-            pltpu.VMEM((kv_heads, n, rows, lanes), bf16),
-            pltpu.VMEM((kv_heads, chunks, 8, lanes), f32),
-            pltpu.VMEM((kv_heads * n * 8, lanes), f32),
+            pltpu.VMEM((n, kv_heads * rows + stat_rows, lanes), bf16),
+            pltpu.VMEM((n, kv_heads * rows + stat_rows, lanes), bf16),
+            pltpu.VMEM((n * stat_rows, lanes), f32),
             pltpu.VMEM((lanes, n), f32),
             pltpu.VMEM((rows, lanes), f32),
             pltpu.VMEM((kv_heads, n, rows, lanes), bf16),
@@ -398,11 +386,8 @@
             pltpu.VMEM((col_tiles, ntp, 2 * block, half), bf16),
             pltpu.VMEM((col_tiles, ntp, 2 * block, half), bf16),
             dma, dma, dma((5,)), dma((4 * kv_heads,)),
-            dma((n,)), dma((n,)),
-            dma((kv_heads, n)), dma((kv_heads, n)),
-            dma((kv_heads, n)), dma((kv_heads, n)),
-            dma((kv_heads, n)), dma((kv_heads, n)),
-            dma((col_tiles, ntp)), dma((col_tiles, ntp)),
+            dma, dma((chunks,)), dma, dma,
+            dma((kv_heads,)), dma((kv_heads,)), dma((col_tiles,)), dma((col_tiles,)),
         ],
         compiler_params=pltpu.CompilerParams(
             collective_id=0, has_side_effects=True, vmem_limit_bytes=56 * 2**20
@@ -425,10 +410,8 @@
     return pl.pallas_call(
         deliver,
         out_shape=out_shape,
-        in_specs=[hbm, hbm],
-        out_specs=(hbm, hbm),
-        scratch_shapes=[dma((2,))],
-        compiler_params=pltpu.CompilerParams(vmem_limit_bytes=60 * 2**20),
+        in_specs=[vmem, vmem],
+        out_specs=(vmem, vmem),
     )(context, projected)
 
 

time: 39.7 us -> 34.9 us (0.88)
  Pallas kernels: 38.9 us -> 34.1 us
    pallas_call x1, Pallas kernels: 35.8 us -> 32.7 us  [per_device(): pl.pallas_call(functools.partial(kernel, n, ntp, local_new, kv_heads, gro...]
    pallas_call x1, Pallas kernels: 3.11 us -> 1.4 us  [per_device(): pl.pallas_call(deliver, out_shape=out_shape, in_specs=[vmem, vmem], out_s...]
where the time goes in v4:
time: 34.9 us; the launch traced here: 34.7 us
  Pallas kernels  34.1 us (98%)
  between operations  0.64 us (2%)
    pallas_call x1, Pallas kernels, per_device(): pl.pallas_call(functools.partial(kernel, n, ntp, local_new, kv_heads, gro...  32.7 us
    pallas_call x1, Pallas kernels, per_device(): pl.pallas_call(deliver, out_shape=out_shape, in_specs=[vmem, vmem], out_s...  1.4 us

profile of v4, /device:TPU:0, one launch (start us, length us, event | category | flops | bytes accessed | tf_op | source)
XLA Modules:
  0.0 34.7 jit_solution(12018182586873887286)
XLA Ops:
  0.6 32.7 %shard_map.95 = (bf16[4,4096]{1,0:T(4,128)(2,1)}, bf16[8,2048]{1,0:T(8,128)(2,1)}) custom-call(bf16[4,32,128]{2,1,0:T(8,128)(2,1)} %q_hbm.1, bf16[4096,128]{1,0:T(8,128)(2,1)} %bitcast.5, bf16[4096,128]{1,0:T(8,128)(2,1)} %bitcast.6, s32[1,2048]{1,0:T(1,128)} %bitcast.7, bf16[8,128]{1,0:T(8,128)(2,1)} %bitcast.8, bf16[8,128]{1,0:T(8,128)(2,1)} %bitcast.9, ...), custom_call_target="tpu_custom_call" | custom-call | flops 1610612736 | bytes 18874368 | tf_op jit(solution)/shard_map/pallas_call | solution.py:357
  33.3 1.4 %shard_map.96 = (bf16[4,4096]{1,0:T(4,128)(2,1)}, bf16[8,2048]{1,0:T(8,128)(2,1)}) custom-call(bf16[4,4096]{1,0:T(4,128)(2,1)} %get-tuple-element.4.ctx_in, bf16[8,2048]{1,0:T(8,128)(2,1)} %get-tuple-element.5.proj_in), custom_call_target="tpu_custom_call" | custom-call | tf_op jit(solution)/shard_map/pallas_call | solution.py:410

commit v5 on v4

--- a/solution.py
+++ b/solution.py
@@ -23,7 +23,7 @@
     q_hbm, k_hbm, v_hbm, pos_hbm, nk_hbm, nv_hbm, newpos_hbm, w_hbm,
     ctx_out, proj_out, pos_ref, nk_ref, nv_ref, newpos_ref,
     kraw, vraw, kh, vh, wide, small, bias_c, bias_n, qall, wbuf,
-    onum, rnum, stat, wts, cown, call, cf, lhs, acc, dsend, drecv,
+    sbuf, pbuf, onum, rnum, stat, wts, cown, call, cf, lhs, acc, dsend, drecv,
     k_sem, v_sem, i_sem, w_sem, q_send, q_recv, n_send, n_recv,
     c_send, c_recv, d_send, d_recv,
 ):
@@ -145,7 +145,7 @@
         lax.fori_loop(1, n, step, 0)
 
     def chunk_at(i, sign):
-        shift = lax.rem(i + chunks // 2 - 2, chunks - 1) + 1
+        shift = lax.rem(i + chunks // 2 - 2 + chunks - 1, chunks - 1) + 1
         return lax.rem(mine + chunks + sign * shift, chunks)
 
     for j in range(1, per_chunk):
@@ -190,33 +190,42 @@
         jnp.int32, (lanes, lanes), 1
     )
 
-    def attend(c, others_of_chunk):
+    def fold(old, new, op):
+        first = op(old[:, :lanes], new)
+        return jnp.concatenate([first, old[:, lanes:]], axis=1)
+
+    def attend(c):
         tok = c * per_chunk * local_new
-        arrivals = len(others_of_chunk) * local_new
-        if arrivals > 0:
-            await_bytes(qall.at[pl.ds(0, arrivals)], q_recv.at[c])
-        scores = []
         for h in range(kv_heads):
             q = qall[pl.ds(tok, per_chunk * local_new), pl.ds(h * group, group), :]
-            scores.append(
-                lax.dot_general(
-                    q.reshape(lanes, lanes), kh[h], (((1,), (1,)), ((), ())),
-                    preferred_element_type=f32,
-                )
+            sbuf[h] = lax.dot_general(
+                q.reshape(lanes, lanes), kh[h], (((1,), (1,)), ((), ())),
+                preferred_element_type=f32,
             )
         levels = jnp.zeros((stat_rows, lanes), f32)
+        blocks = lanes // 16
         for h in range(kv_heads):
-            s = scores[h]
-            old = s[:, :slots] + bias_c[...]
-            new = s[:, slots:] + bias_n[pl.ds(tok * group, lanes), :]
-            top = jnp.maximum(
-                jnp.max(old, axis=1, keepdims=True), jnp.max(new, axis=1, keepdims=True)
-            )
-            old = jnp.exp2((old - top) * coef)
-            new = jnp.exp2((new - top) * coef)
-            total = jnp.sum(old, axis=1, keepdims=True) + jnp.sum(new, axis=1, keepdims=True)
-            out = jnp.dot(old.astype(bf16), vh[h, :slots], preferred_element_type=f32)
-            out += jnp.dot(new.astype(bf16), vh[h, slots:], preferred_element_type=f32)
+
+            def masked(b):
+                at = pl.ds(b * 16, 16)
+                old = sbuf[h, at, :slots] + bias_c[...]
+                new = sbuf[h, at, slots:] + bias_n[pl.ds(tok * group + b * 16, 16), :]
+                return old, new
+
+            tops = []
+            for b in range(blocks):
+                tops.append(jnp.max(fold(*masked(b), jnp.maximum), axis=1, keepdims=True))
+            totals = []
+            for b in range(blocks):
+                old, new = masked(b)
+                old = jnp.exp2((old - tops[b]) * coef)
+                new = jnp.exp2((new - tops[b]) * coef)
+                totals.append(jnp.sum(fold(old, new, jnp.add), axis=1, keepdims=True))
+                pbuf[h, b * 16 : (b + 1) * 16, :slots] = old.astype(bf16)
+                pbuf[h, b * 16 : (b + 1) * 16, slots:] = new.astype(bf16)
+            top = jnp.concatenate(tops, axis=0)
+            total = jnp.concatenate(totals, axis=0)
+            out = jnp.dot(pbuf[h], vh[h], preferred_element_type=f32)
             out = (out / total).astype(bf16)
             level = top * coef + jnp.log2(total)
             level = jnp.sum(jnp.where(diag, level, 0.0), axis=0, keepdims=True)
@@ -230,24 +239,37 @@
                 ]
         for j in range(per_chunk):
             onum[c * per_chunk + j, num_rows:] = levels.astype(bf16)
-        for peer in others_of_chunk:
-            num_copy(peer).start()
 
     def attend_all():
-        attend(
-            mine,
-            [
-                mine * per_chunk + lax.rem(me + j, per_chunk) for j in range(1, per_chunk)
-            ],
-        )
-        rnum[me] = onum[me]
-
         def step(i, _):
-            c = chunk_at(i, -1)
-            attend(c, [c * per_chunk + j for j in range(per_chunk)])
+            c = jnp.where(i == 0, mine, chunk_at(i, -1))
+
+            @pl.when(i > 0)
+            def _():
+                await_bytes(qall.at[pl.ds(0, per_chunk * local_new)], q_recv.at[c])
+
+            if per_chunk > 1:
+
+                @pl.when(i == 0)
+                def _():
+                    await_bytes(qall.at[pl.ds(0, (per_chunk - 1) * local_new)], q_recv.at[c])
+
+            attend(c)
+
+            @pl.when(i > 0)
+            def _():
+                for j in range(per_chunk):
+                    num_copy(c * per_chunk + j).start()
+
+            @pl.when(i == 0)
+            def _():
+                for j in range(1, per_chunk):
+                    num_copy(c * per_chunk + lax.rem(me + j, per_chunk)).start()
+                rnum[me] = onum[me]
+
             return 0
 
-        lax.fori_loop(1, chunks, step, 0)
+        lax.fori_loop(0, chunks, step, 0)
 
     def combine(h):
         level = stat[pl.ds(3 * h, n, stride=stat_rows), :]
@@ -374,6 +396,8 @@
             pltpu.VMEM((tokens * group, lanes), f32),
             pltpu.VMEM((tokens, heads, lanes), bf16),
             pltpu.VMEM((depth, cols), bf16),
+            pltpu.VMEM((kv_heads, lanes, all_keys), f32),
+            pltpu.VMEM((kv_heads, lanes, all_keys), bf16),
             pltpu.VMEM((n, kv_heads * rows + stat_rows, lanes), bf16),
             pltpu.VMEM((n, kv_heads * rows + stat_rows, lanes), bf16),
             pltpu.VMEM((n * stat_rows, lanes), f32),

time: 34.9 us -> 35.3 us (1.011)
  Pallas kernels: 34.1 us -> 34.5 us
    pallas_call x1, Pallas kernels: 32.7 us -> 33.1 us  [per_device(): pl.pallas_call(functools.partial(kernel, n, ntp, local_new, kv_heads, gro...]
where the time goes in v5:
time: 35.3 us; the launch traced here: 35.1 us
  Pallas kernels  34.5 us (98%)
  between operations  0.64 us (2%)
    pallas_call x1, Pallas kernels, per_device(): pl.pallas_call(functools.partial(kernel, n, ntp, local_new, kv_heads, gro...  33.1 us
    pallas_call x1, Pallas kernels, per_device(): pl.pallas_call(deliver, out_shape=out_shape, in_specs=[vmem, vmem], out_s...  1.4 us

profile of v5, /device:TPU:0, one launch (start us, length us, event | category | flops | bytes accessed | tf_op | source)
XLA Modules:
  0.0 35.1 jit_solution(10539350588665867071)
XLA Ops:
  0.6 33.1 %shard_map.95 = (bf16[4,4096]{1,0:T(4,128)(2,1)}, bf16[8,2048]{1,0:T(8,128)(2,1)}) custom-call(bf16[4,32,128]{2,1,0:T(8,128)(2,1)} %q_hbm.1, bf16[4096,128]{1,0:T(8,128)(2,1)} %bitcast.5, bf16[4096,128]{1,0:T(8,128)(2,1)} %bitcast.6, s32[1,2048]{1,0:T(1,128)} %bitcast.7, bf16[8,128]{1,0:T(8,128)(2,1)} %bitcast.8, bf16[8,128]{1,0:T(8,128)(2,1)} %bitcast.9, ...), custom_call_target="tpu_custom_call" | custom-call | flops 1610612736 | bytes 18874368 | tf_op jit(solution)/shard_map/pallas_call | solution.py:379
  33.7 1.4 %shard_map.96 = (bf16[4,4096]{1,0:T(4,128)(2,1)}, bf16[8,2048]{1,0:T(8,128)(2,1)}) custom-call(bf16[4,4096]{1,0:T(4,128)(2,1)} %get-tuple-element.4.ctx_in, bf16[8,2048]{1,0:T(8,128)(2,1)} %get-tuple-element.5.proj_in), custom_call_target="tpu_custom_call" | custom-call | tf_op jit(solution)/shard_map/pallas_call | solution.py:434

commit v6 on v4

--- a/solution.py
+++ b/solution.py
@@ -33,7 +33,6 @@
     per_chunk = lanes // rows
     chunks = n // per_chunk
     mine = me // per_chunk
-    num_rows = kv_heads * rows
     tokens = n * local_new
     depth = group * lanes
     coef = math.log2(math.e) / math.sqrt(lanes)
@@ -94,22 +93,23 @@
 
     pl.semaphore_wait(barrier, n - 1 + ntp - 1)
 
-    def q_copy(peer):
+    def q_copy(h, peer):
+        heads = pl.ds(h * group, group)
         return pltpu.make_async_remote_copy(
-            src_ref=q_hbm,
-            dst_ref=qall.at[pl.ds(me * local_new, local_new)],
+            src_ref=q_hbm.at[:, heads],
+            dst_ref=qall.at[pl.ds(me * local_new, local_new), heads],
             send_sem=q_send,
-            recv_sem=q_recv.at[mine],
+            recv_sem=q_recv.at[h, mine],
             device_id={"ctx": peer},
             device_id_type=MESH,
         )
 
-    def num_copy(peer):
+    def num_copy(h, peer):
         return pltpu.make_async_remote_copy(
-            src_ref=onum.at[peer],
-            dst_ref=rnum.at[me],
-            send_sem=n_send,
-            recv_sem=n_recv,
+            src_ref=onum.at[h, peer],
+            dst_ref=rnum.at[h, me],
+            send_sem=n_send.at[h],
+            recv_sem=n_recv.at[h],
             device_id={"ctx": peer},
             device_id_type=MESH,
         )
@@ -148,16 +148,17 @@
         shift = lax.rem(i + chunks // 2 - 2, chunks - 1) + 1
         return lax.rem(mine + chunks + sign * shift, chunks)
 
-    for j in range(1, per_chunk):
-        q_copy(mine * per_chunk + lax.rem(me + j, per_chunk)).start()
-
-    def send_queries(i, _):
-        c = chunk_at(i, 1)
-        for j in range(per_chunk):
-            q_copy(c * per_chunk + j).start()
-        return 0
-
-    lax.fori_loop(1, chunks, send_queries, 0)
+    for h in range(kv_heads):
+        for j in range(1, per_chunk):
+            q_copy(h, mine * per_chunk + lax.rem(me + j, per_chunk)).start()
+
+        def send_queries(i, _):
+            c = chunk_at(i, 1)
+            for j in range(per_chunk):
+                q_copy(h, c * per_chunk + j).start()
+            return 0
+
+        lax.fori_loop(1, chunks, send_queries, 0)
 
     part = math.gcd(slots, 512)
 
@@ -190,69 +191,62 @@
         jnp.int32, (lanes, lanes), 1
     )
 
-    def attend(c, others_of_chunk):
+    def attend(h, c, others_of_chunk):
         tok = c * per_chunk * local_new
+        heads = pl.ds(h * group, group)
         arrivals = len(others_of_chunk) * local_new
         if arrivals > 0:
-            await_bytes(qall.at[pl.ds(0, arrivals)], q_recv.at[c])
-        scores = []
-        for h in range(kv_heads):
-            q = qall[pl.ds(tok, per_chunk * local_new), pl.ds(h * group, group), :]
-            scores.append(
-                lax.dot_general(
-                    q.reshape(lanes, lanes), kh[h], (((1,), (1,)), ((), ())),
-                    preferred_element_type=f32,
-                )
-            )
+            await_bytes(qall.at[pl.ds(0, arrivals), heads], q_recv.at[h, c])
+        q = qall[pl.ds(tok, per_chunk * local_new), heads, :].reshape(lanes, lanes)
+        s = lax.dot_general(
+            q, kh[h], (((1,), (1,)), ((), ())), preferred_element_type=f32
+        )
+        old = s[:, :slots] + bias_c[...]
+        new = s[:, slots:] + bias_n[pl.ds(tok * group, lanes), :]
+        top = jnp.maximum(
+            jnp.max(old, axis=1, keepdims=True), jnp.max(new, axis=1, keepdims=True)
+        )
+        old = jnp.exp2((old - top) * coef)
+        new = jnp.exp2((new - top) * coef)
+        total = jnp.sum(old, axis=1, keepdims=True) + jnp.sum(new, axis=1, keepdims=True)
+        out = jnp.dot(old.astype(bf16), vh[h, :slots], preferred_element_type=f32)
+        out += jnp.dot(new.astype(bf16), vh[h, slots:], preferred_element_type=f32)
+        out = (out / total).astype(bf16)
+        level = top * coef + jnp.log2(total)
+        level = jnp.sum(jnp.where(diag, level, 0.0), axis=0, keepdims=True)
         levels = jnp.zeros((stat_rows, lanes), f32)
-        for h in range(kv_heads):
-            s = scores[h]
-            old = s[:, :slots] + bias_c[...]
-            new = s[:, slots:] + bias_n[pl.ds(tok * group, lanes), :]
-            top = jnp.maximum(
-                jnp.max(old, axis=1, keepdims=True), jnp.max(new, axis=1, keepdims=True)
-            )
-            old = jnp.exp2((old - top) * coef)
-            new = jnp.exp2((new - top) * coef)
-            total = jnp.sum(old, axis=1, keepdims=True) + jnp.sum(new, axis=1, keepdims=True)
-            out = jnp.dot(old.astype(bf16), vh[h, :slots], preferred_element_type=f32)
-            out += jnp.dot(new.astype(bf16), vh[h, slots:], preferred_element_type=f32)
-            out = (out / total).astype(bf16)
-            level = top * coef + jnp.log2(total)
-            level = jnp.sum(jnp.where(diag, level, 0.0), axis=0, keepdims=True)
-            for k in range(3):
-                piece = level.astype(bf16).astype(f32)
-                level = level - piece
-                levels = jnp.where(stat_row == 3 * h + k, piece, levels)
-            for j in range(per_chunk):
-                onum[c * per_chunk + j, h * rows : (h + 1) * rows] = out[
-                    j * rows : (j + 1) * rows
-                ]
+        for k in range(3):
+            piece = level.astype(bf16).astype(f32)
+            level = level - piece
+            levels = jnp.where(stat_row == k, piece, levels)
         for j in range(per_chunk):
-            onum[c * per_chunk + j, num_rows:] = levels.astype(bf16)
+            onum[h, c * per_chunk + j, :rows] = out[j * rows : (j + 1) * rows]
+            onum[h, c * per_chunk + j, rows:] = levels.astype(bf16)
         for peer in others_of_chunk:
-            num_copy(peer).start()
-
-    def attend_all():
+            num_copy(h, peer).start()
+
+    def attend_all(h):
         attend(
-            mine,
+            h, mine,
             [
                 mine * per_chunk + lax.rem(me + j, per_chunk) for j in range(1, per_chunk)
             ],
         )
-        rnum[me] = onum[me]
+        rnum[h, me] = onum[h, me]
 
         def step(i, _):
             c = chunk_at(i, -1)
-            attend(c, [c * per_chunk + j for j in range(per_chunk)])
+            attend(h, c, [c * per_chunk + j for j in range(per_chunk)])
             return 0
 
         lax.fori_loop(1, chunks, step, 0)
 
     def combine(h):
-        level = stat[pl.ds(3 * h, n, stride=stat_rows), :]
+        await_bytes(rnum.at[h, pl.ds(0, n - 1)], n_recv.at[h])
+        stat[...] = rnum[h, :, rows:, :].reshape(n * stat_rows, lanes).astype(f32)
+        level = stat[pl.ds(0, n, stride=stat_rows), :]
         for k in range(1, 3):
-            level += stat[pl.ds(3 * h + k, n, stride=stat_rows), :]
+            level += stat[pl.ds(k, n, stride=stat_rows), :]
         factor = jnp.exp2(level - jnp.max(level, axis=0, keepdims=True))
         factor = factor / jnp.sum(factor, axis=0, keepdims=True)
         wts[...] = factor.T
@@ -260,7 +254,7 @@
         weight = wts[pl.ds(first, rows), :]
         context = jnp.zeros((rows, lanes), f32)
         for s in range(n):
-            context += rnum[s, h * rows : (h + 1) * rows].astype(f32) * weight[:, s : s + 1]
+            context += rnum[h, s, :rows].astype(f32) * weight[:, s : s + 1]
         call[h, me] = context.astype(bf16)
         others(lambda peer: ctx_copy(h, peer).start())
         cown[...] = context
@@ -302,9 +296,8 @@
                 def _():
                     drecv[j, tp] = slab
 
-    attend_all()
-    await_bytes(rnum.at[pl.ds(0, n - 1)], n_recv)
-    stat[...] = rnum[:, num_rows:, :].reshape(n * stat_rows, lanes).astype(f32)
+    for h in range(kv_heads):
+        attend_all(h)
     for h in range(kv_heads):
         combine(h)
     for h in range(kv_heads):
@@ -320,8 +313,8 @@
         ).astype(bf16)
 
     await_bytes(qall.at[pl.ds(0, (n - 1) * local_new)], q_send)
-    await_bytes(onum.at[pl.ds(0, n - 1)], n_send)
     for h in range(kv_heads):
+        await_bytes(onum.at[h, pl.ds(0, n - 1)], n_send.at[h])
         await_bytes(call.at[h, pl.ds(0, n - 1)], c_send.at[h])
     for j in range(col_tiles):
         await_bytes(dsend.at[j, pl.ds(0, ntp - 1)], d_send.at[j])
@@ -374,8 +367,8 @@
             pltpu.VMEM((tokens * group, lanes), f32),
             pltpu.VMEM((tokens, heads, lanes), bf16),
             pltpu.VMEM((depth, cols), bf16),
-            pltpu.VMEM((n, kv_heads * rows + stat_rows, lanes), bf16),
-            pltpu.VMEM((n, kv_heads * rows + stat_rows, lanes), bf16),
+            pltpu.VMEM((kv_heads, n, rows + stat_rows, lanes), bf16),
+            pltpu.VMEM((kv_heads, n, rows + stat_rows, lanes), bf16),
             pltpu.VMEM((n * stat_rows, lanes), f32),
             pltpu.VMEM((lanes, n), f32),
             pltpu.VMEM((rows, lanes), f32),
@@ -386,7 +379,7 @@
             pltpu.VMEM((col_tiles, ntp, 2 * block, half), bf16),
             pltpu.VMEM((col_tiles, ntp, 2 * block, half), bf16),
             dma, dma, dma((5,)), dma((4 * kv_heads,)),
-            dma, dma((chunks,)), dma, dma,
+            dma, dma((kv_heads, chunks)), dma((kv_heads,)), dma((kv_heads,)),
             dma((kv_heads,)), dma((kv_heads,)), dma((col_tiles,)), dma((col_tiles,)),
         ],
         compiler_params=pltpu.CompilerParams(

time: 34.9 us -> 35 us (level)
  no operation moved by 1% of the time
where the time goes in v6:
time: 35 us; the launch traced here: 34.8 us
  Pallas kernels  34.1 us (97%)
  between operations  0.64 us (2%)
    pallas_call x1, Pallas kernels, per_device(): pl.pallas_call(functools.partial(kernel, n, ntp, local_new, kv_heads, gro...  32.7 us
    pallas_call x1, Pallas kernels, per_device(): pl.pallas_call(deliver, out_shape=out_shape, in_specs=[vmem, vmem], out_s...  1.4 us

profile of v6, /device:TPU:0, one launch (start us, length us, event | category | flops | bytes accessed | tf_op | source)
XLA Modules:
  0.0 34.8 jit_solution(18067118837355791046)
XLA Ops:
  0.6 32.7 %shard_map.95 = (bf16[4,4096]{1,0:T(4,128)(2,1)}, bf16[8,2048]{1,0:T(8,128)(2,1)}) custom-call(bf16[4,32,128]{2,1,0:T(8,128)(2,1)} %q_hbm.1, bf16[4096,128]{1,0:T(8,128)(2,1)} %bitcast.5, bf16[4096,128]{1,0:T(8,128)(2,1)} %bitcast.6, s32[1,2048]{1,0:T(1,128)} %bitcast.7, bf16[8,128]{1,0:T(8,128)(2,1)} %bitcast.8, bf16[8,128]{1,0:T(8,128)(2,1)} %bitcast.9, ...), custom_call_target="tpu_custom_call" | custom-call | flops 1610612736 | bytes 18874368 | tf_op jit(solution)/shard_map/pallas_call | solution.py:350
  33.4 1.4 %shard_map.96 = (bf16[4,4096]{1,0:T(4,128)(2,1)}, bf16[8,2048]{1,0:T(8,128)(2,1)}) custom-call(bf16[4,4096]{1,0:T(4,128)(2,1)} %get-tuple-element.4.ctx_in, bf16[8,2048]{1,0:T(8,128)(2,1)} %get-tuple-element.5.proj_in), custom_call_target="tpu_custom_call" | custom-call | tf_op jit(solution)/shard_map/pallas_call | solution.py:403

commit v7 on v6

--- a/solution.py
+++ b/solution.py
@@ -191,18 +191,24 @@
         jnp.int32, (lanes, lanes), 1
     )
 
-    def attend(h, c, others_of_chunk):
-        tok = c * per_chunk * local_new
+    def attend(h, pair):
         heads = pl.ds(h * group, group)
-        arrivals = len(others_of_chunk) * local_new
-        if arrivals > 0:
-            await_bytes(qall.at[pl.ds(0, arrivals), heads], q_recv.at[h, c])
-        q = qall[pl.ds(tok, per_chunk * local_new), heads, :].reshape(lanes, lanes)
+        qs, news = [], []
+        for c, others_of_chunk in pair:
+            tok = c * per_chunk * local_new
+            arrivals = len(others_of_chunk) * local_new
+            if arrivals > 0:
+                await_bytes(qall.at[pl.ds(0, arrivals), heads], q_recv.at[h, c])
+        for c, _ in pair:
+            tok = c * per_chunk * local_new
+            qs.append(qall[pl.ds(tok, per_chunk * local_new), heads, :].reshape(lanes, lanes))
+            news.append(bias_n[pl.ds(tok * group, lanes), :])
         s = lax.dot_general(
-            q, kh[h], (((1,), (1,)), ((), ())), preferred_element_type=f32
+            jnp.concatenate(qs, axis=0), kh[h], (((1,), (1,)), ((), ())),
+            preferred_element_type=f32,
         )
         old = s[:, :slots] + bias_c[...]
-        new = s[:, slots:] + bias_n[pl.ds(tok * group, lanes), :]
+        new = s[:, slots:] + jnp.concatenate(news, axis=0)
         top = jnp.maximum(
             jnp.max(old, axis=1, keepdims=True), jnp.max(new, axis=1, keepdims=True)
         )
@@ -212,34 +218,38 @@
         out = jnp.dot(old.astype(bf16), vh[h, :slots], preferred_element_type=f32)
         out += jnp.dot(new.astype(bf16), vh[h, slots:], preferred_element_type=f32)
         out = (out / total).astype(bf16)
-        level = top * coef + jnp.log2(total)
-        level = jnp.sum(jnp.where(diag, level, 0.0), axis=0, keepdims=True)
-        levels = jnp.zeros((stat_rows, lanes), f32)
-        for k in range(3):
-            piece = level.astype(bf16).astype(f32)
-            level = level - piece
-            levels = jnp.where(stat_row == k, piece, levels)
-        for j in range(per_chunk):
-            onum[h, c * per_chunk + j, :rows] = out[j * rows : (j + 1) * rows]
-            onum[h, c * per_chunk + j, rows:] = levels.astype(bf16)
-        for peer in others_of_chunk:
-            num_copy(h, peer).start()
-
-    def attend_all(h):
-        attend(
-            h, mine,
-            [
-                mine * per_chunk + lax.rem(me + j, per_chunk) for j in range(1, per_chunk)
-            ],
-        )
+        levels_all = top * coef + jnp.log2(total)
+        for i, (c, others_of_chunk) in enumerate(pair):
+            level = levels_all[i * lanes : (i + 1) * lanes]
+            level = jnp.sum(jnp.where(diag, level, 0.0), axis=0, keepdims=True)
+            levels = jnp.zeros((stat_rows, lanes), f32)
+            for k in range(3):
+                piece = level.astype(bf16).astype(f32)
+                level = level - piece
+                levels = jnp.where(stat_row == k, piece, levels)
+            for j in range(per_chunk):
+                at = i * lanes + j * rows
+                onum[h, c * per_chunk + j, :rows] = out[at : at + rows]
+                onum[h, c * per_chunk + j, rows:] = levels.astype(bf16)
+        for c, others_of_chunk in reversed(pair):
+            for peer in others_of_chunk:
+                num_copy(h, peer).start()
+
+    def whole_chunk(i):
+        c = chunk_at(i, -1)
+        return c, [c * per_chunk + j for j in range(per_chunk)]
+
+    def attend_first(h):
+        mates = [mine * per_chunk + lax.rem(me + j, per_chunk) for j in range(1, per_chunk)]
+        attend(h, [(mine, mates), whole_chunk(1)])
         rnum[h, me] = onum[h, me]
 
+    def attend_rest(h):
         def step(i, _):
-            c = chunk_at(i, -1)
-            attend(h, c, [c * per_chunk + j for j in range(per_chunk)])
+            attend(h, [whole_chunk(2 * i), whole_chunk(2 * i + 1)])
             return 0
 
-        lax.fori_loop(1, chunks, step, 0)
+        lax.fori_loop(1, chunks // 2, step, 0)
 
     def combine(h):
         await_bytes(rnum.at[h, pl.ds(0, n - 1)], n_recv.at[h])
@@ -297,9 +307,11 @@
                     drecv[j, tp] = slab
 
     for h in range(kv_heads):
-        attend_all(h)
-    for h in range(kv_heads):
-        combine(h)
+        attend_first(h)
+        if h > 0:
+            combine(h - 1)
+        attend_rest(h)
+    combine(kv_heads - 1)
     for h in range(kv_heads):
         project(h)
 

time: 35 us -> 38.7 us (1.11)
  Pallas kernels: 34.1 us -> 37.9 us
    pallas_call x1, Pallas kernels: 32.7 us -> 36.5 us  [per_device(): pl.pallas_call(functools.partial(kernel, n, ntp, local_new, kv_heads, gro...]
where the time goes in v7:
time: 38.7 us; the launch traced here: 38.5 us
  Pallas kernels  37.9 us (98%)
  between operations  0.64 us (2%)
    pallas_call x1, Pallas kernels, per_device(): pl.pallas_call(functools.partial(kernel, n, ntp, local_new, kv_heads, gro...  36.5 us
    pallas_call x1, Pallas kernels, per_device(): pl.pallas_call(deliver, out_shape=out_shape, in_specs=[vmem, vmem], out_s...  1.4 us

profile of v7, /device:TPU:0, one launch (start us, length us, event | category | flops | bytes accessed | tf_op | source)
XLA Modules:
  0.0 38.5 jit_solution(5481106456404234394)
XLA Ops:
  0.6 36.5 %shard_map.95 = (bf16[4,4096]{1,0:T(4,128)(2,1)}, bf16[8,2048]{1,0:T(8,128)(2,1)}) custom-call(bf16[4,32,128]{2,1,0:T(8,128)(2,1)} %q_hbm.1, bf16[4096,128]{1,0:T(8,128)(2,1)} %bitcast.5, bf16[4096,128]{1,0:T(8,128)(2,1)} %bitcast.6, s32[1,2048]{1,0:T(1,128)} %bitcast.7, bf16[8,128]{1,0:T(8,128)(2,1)} %bitcast.8, bf16[8,128]{1,0:T(8,128)(2,1)} %bitcast.9, ...), custom_call_target="tpu_custom_call" | custom-call | flops 1610612736 | bytes 18874368 | tf_op jit(solution)/shard_map/pallas_call | solution.py:362
  37.1 1.4 %shard_map.96 = (bf16[4,4096]{1,0:T(4,128)(2,1)}, bf16[8,2048]{1,0:T(8,128)(2,1)}) custom-call(bf16[4,4096]{1,0:T(4,128)(2,1)} %get-tuple-element.4.ctx_in, bf16[8,2048]{1,0:T(8,128)(2,1)} %get-tuple-element.5.proj_in), custom_call_target="tpu_custom_call" | custom-call | tf_op jit(solution)/shard_map/pallas_call | solution.py:415

commit v8 on v4

--- a/solution.py
+++ b/solution.py
@@ -76,22 +76,6 @@
         pl.semaphore_signal(
             barrier, inc=1, device_id={"tp": lax.rem(tp + i, ntp)}, device_id_type=MESH
         )
-    for copy in small_copies:
-        copy.wait()
-    bias_c[...] = jnp.where(pos_ref[...] >= 0, 0.0, masked_score)
-    lane = lax.broadcasted_iota(jnp.int32, (group, lanes), 1)
-    key_pos = jnp.full((group, lanes), 2**30, jnp.int32)
-    for j in range(local_new):
-        key_pos = jnp.where(lane == j, newpos_ref[me * local_new + j], key_pos)
-
-    def mask_new(t, _):
-        bias_n[pl.ds(t * group, group), :] = jnp.where(
-            key_pos <= newpos_ref[t], 0.0, masked_score
-        )
-        return 0
-
-    lax.fori_loop(0, tokens, mask_new, 0)
-
     pl.semaphore_wait(barrier, n - 1 + ntp - 1)
 
     def q_copy(peer):
@@ -158,6 +142,22 @@
         return 0
 
     lax.fori_loop(1, chunks, send_queries, 0)
+
+    for copy in small_copies:
+        copy.wait()
+    bias_c[...] = jnp.where(pos_ref[...] >= 0, 0.0, masked_score)
+    lane = lax.broadcasted_iota(jnp.int32, (group, lanes), 1)
+    key_pos = jnp.full((group, lanes), 2**30, jnp.int32)
+    for j in range(local_new):
+        key_pos = jnp.where(lane == j, newpos_ref[me * local_new + j], key_pos)
+
+    def mask_new(t, _):
+        bias_n[pl.ds(t * group, group), :] = jnp.where(
+            key_pos <= newpos_ref[t], 0.0, masked_score
+        )
+        return 0
+
+    lax.fori_loop(0, tokens, mask_new, 0)
 
     part = math.gcd(slots, 512)
 

time: 34.9 us -> 34.9 us (level)
  no operation moved by 1% of the time
where the time goes in v8:
time: 34.9 us; the launch traced here: 34.7 us
  Pallas kernels  34.1 us (98%)
  between operations  0.64 us (2%)
    pallas_call x1, Pallas kernels, per_device(): pl.pallas_call(functools.partial(kernel, n, ntp, local_new, kv_heads, gro...  32.7 us
    pallas_call x1, Pallas kernels, per_device(): pl.pallas_call(deliver, out_shape=out_shape, in_specs=[vmem, vmem], out_s...  1.4 us

profile of v8, /device:TPU:0, one launch (start us, length us, event | category | flops | bytes accessed | tf_op | source)
XLA Modules:
  0.0 34.7 jit_solution(13247274905816684507)
XLA Ops:
  0.6 32.7 %shard_map.95 = (bf16[4,4096]{1,0:T(4,128)(2,1)}, bf16[8,2048]{1,0:T(8,128)(2,1)}) custom-call(bf16[4,32,128]{2,1,0:T(8,128)(2,1)} %q_hbm.1, bf16[4096,128]{1,0:T(8,128)(2,1)} %bitcast.5, bf16[4096,128]{1,0:T(8,128)(2,1)} %bitcast.6, s32[1,2048]{1,0:T(1,128)} %bitcast.7, bf16[8,128]{1,0:T(8,128)(2,1)} %bitcast.8, bf16[8,128]{1,0:T(8,128)(2,1)} %bitcast.9, ...), custom_call_target="tpu_custom_call" | custom-call | flops 1610612736 | bytes 18874368 | tf_op jit(solution)/shard_map/pallas_call | solution.py:357
  33.3 1.4 %shard_map.96 = (bf16[4,4096]{1,0:T(4,128)(2,1)}, bf16[8,2048]{1,0:T(8,128)(2,1)}) custom-call(bf16[4,4096]{1,0:T(4,128)(2,1)} %get-tuple-element.4.ctx_in, bf16[8,2048]{1,0:T(8,128)(2,1)} %get-tuple-element.5.proj_in), custom_call_target="tpu_custom_call" | custom-call | tf_op jit(solution)/shard_map/pallas_call | solution.py:410
